TPU v7x, 256 devices: a whole 4x4x8 slice. The times are simulated.
256 devices in a mesh: slab: 32 (over x, z_lo, core), kgrp: 8 (over y, z_hi).
Axes of the slice: x: 4, y: 4, z: 8 (z_hi: 2, z_lo: 4; z = z_hi * 4 + z_lo), core: 2. Of those that a mesh axis runs over, the one named last changes fastest.
Arguments:
- atom_descriptors: bfloat16 [32768, 128], P(('slab', 'kgrp')), may hold values from -6 to 6
- atom_locations: float32 [3, 32768], P(None, ('slab', 'kgrp')), may hold values from 0 to 32, as said below
- adjacent_atom_slots: int32 [32768, 64], P(('slab', 'kgrp')), may hold values from 0 to 3071
- neighbour_tally: int32 [32768], P(('slab', 'kgrp')), may hold values from 16 to 64
- filled_slot_tallies: int32 [32], replicated, may hold values from 1 to 1024, 24576 in all
- reciprocal_lattice_modes: float32 [3, 8192], P(None, 'kgrp'), may hold values from -4 to 4
- edge_update_matrix: bfloat16 [2, 128, 128], replicated, may hold values from -0.5 to 0.5
- node_update_matrix: bfloat16 [2, 128, 128], replicated, may hold values from -0.5 to 0.5
- distance_basis_mixing: float32 [2, 8, 128], replicated, may hold values from -2 to 2
- latent_ionic_readout: bfloat16 [128, 16], replicated, may hold values from -0.5 to 0.5
Outputs:
- potential: float32 [16, 32768], P(None, ('slab', 'kgrp'))
- forces: float32 [3, 32768], P(None, ('slab', 'kgrp'))
Inputs may be any that keep to these rules, and one draw needn't show every extreme that they name: `atom_locations`: coordinates of atoms of slab s: first in [s, s+1), others in [0, 1).
All inputs are finite; a program needn't handle non-finite values.
Results may differ from a plain program's by a relative error of at most 0.0028.
Values may be sent and summed in bfloat16 or wider, within the bound.
No kernel may reach another device: no remote copies, remote signals or barrier semaphores. Data moves between devices by JAX's collectives and lax.ppermute only.
A program may use at most 64 MiB of HBM per device.

v0:
```python
import math

import jax
import jax.numpy as jnp
from jax import lax
from jax.sharding import PartitionSpec as P


def extended(cells, sides, width):
    for axis, dim in sides:
        count = lax.axis_size(axis)
        head = lax.slice_in_dim(cells, 0, width, axis=dim)
        tail = lax.slice_in_dim(cells, cells.shape[dim] - width, cells.shape[dim], axis=dim)
        cells = jnp.concatenate(
            [
                lax.ppermute(tail, axis, [(i, (i + 1) % count) for i in range(count)]),
                cells,
                lax.ppermute(head, axis, [((i + 1) % count, i) for i in range(count)]),
            ],
            axis=dim,
        )
    return cells


def bessel_basis(offsets, box_length, count):
    wrapped = jnp.where(offsets[0] > 0.5 * box_length, offsets[0] - box_length, offsets[0])
    wrapped = jnp.where(wrapped < -0.5 * box_length, wrapped + box_length, wrapped)
    distance = jnp.sqrt(
        wrapped * wrapped + offsets[1] * offsets[1] + offsets[2] * offsets[2] + 0.04
    )
    orders = jnp.arange(1, count + 1).astype(jnp.float32).reshape((count,) + (1,) * distance.ndim)
    return math.sqrt(2.0 / 3.0) * jnp.sin(orders * (math.pi / 3.0) * distance) / distance


def interact(hidden, gathered_rows, basis, usable, rad_weight, self_weight):
    radial = jnp.einsum("bae,bc->aec", basis, rad_weight, precision=lax.Precision.HIGHEST)
    terms = radial * gathered_rows.astype(jnp.float32)
    summed = jnp.sum(jnp.where(usable[:, :, None], terms, 0.0), axis=1) * 0.125
    self_term = jnp.dot(hidden, self_weight, preferred_element_type=jnp.float32)
    return (hidden.astype(jnp.float32) + jax.nn.silu(summed + self_term)).astype(jnp.bfloat16)


def maximum_entry(left, right):
    return jnp.dot(left, right, precision=lax.Precision.HIGHEST, preferred_element_type=jnp.float32)


def ewald_screening_coef(mode_batch_index, prefactor_scale):
    mode_norm_square = jnp.sum(mode_batch_index * mode_batch_index, axis=0)
    return prefactor_scale * jnp.exp(-mode_norm_square / 8.0) / (mode_norm_square + 1.0)


def respond(
    cosine_terms,
    sine_terms,
    charges,
    real_component,
    imaginary_component,
    mode_batch_index,
    mode_ewald_coefficient,
):
    weighted_real = mode_ewald_coefficient[:, None] * real_component
    weighted_imag = mode_ewald_coefficient[:, None] * imaginary_component
    potential_part = maximum_entry(cosine_terms, weighted_real) + maximum_entry(
        sine_terms, weighted_imag
    )
    real_drive = maximum_entry(charges, weighted_real.T)
    imag_drive = maximum_entry(charges, weighted_imag.T)
    gradient_k = imag_drive * cosine_terms - real_drive * sine_terms
    forces_part = -maximum_entry(gradient_k, mode_batch_index.T)
    return (potential_part.T, forces_part.T)


def shards(
    atom_descriptors,
    atom_locations,
    adjacent_atom_slots,
    neighbour_tally,
    filled_slot_tallies,
    reciprocal_lattice_modes,
    edge_update_matrix,
    node_update_matrix,
    distance_basis_mixing,
    latent_ionic_readout,
):
    n_slab = lax.axis_size("slab")
    mode_batch_number = lax.axis_size("kgrp")
    slab_idx = lax.axis_index("slab")
    group_idx = lax.axis_index("kgrp")
    atoms_here = atom_descriptors.shape[0]
    slab_rows = atoms_here * mode_batch_number
    box_length = float(n_slab)
    local_rows = group_idx * atoms_here + jnp.arange(atoms_here, dtype=jnp.int32)
    occupied = local_rows < filled_slot_tallies[slab_idx]
    regions = jnp.arange(3, dtype=jnp.int32)
    counts = jnp.take(filled_slot_tallies, (slab_idx + regions - 1) % n_slab)
    occupied_ext = (jnp.arange(slab_rows, dtype=jnp.int32)[None, :] < counts[:, None]).reshape(-1)
    layer_cell_locations = lax.all_gather(atom_locations, "kgrp", axis=1, tiled=True)
    pos_ext = extended(layer_cell_locations, (("slab", 1),), slab_rows)
    offsets = jnp.take(pos_ext, adjacent_atom_slots, axis=1) - atom_locations[:, :, None]
    basis = bessel_basis(offsets, box_length, distance_basis_mixing.shape[1])
    slot_ids = jnp.arange(adjacent_atom_slots.shape[1], dtype=jnp.int32)
    usable = (
        (slot_ids[None, :] < neighbour_tally[:, None])
        & jnp.take(occupied_ext, adjacent_atom_slots)
        & occupied[:, None]
    )
    hidden = atom_descriptors
    for layer_idx in range(edge_update_matrix.shape[0]):
        message_rows = jnp.dot(
            hidden, edge_update_matrix[layer_idx], preferred_element_type=jnp.float32
        ).astype(jnp.bfloat16)
        slab_messages = lax.all_gather(message_rows, "kgrp", axis=0, tiled=True)
        ext_messages = extended(slab_messages, (("slab", 0),), slab_rows)
        hidden = interact(
            hidden,
            jnp.take(ext_messages, adjacent_atom_slots, axis=0),
            basis,
            usable,
            distance_basis_mixing[layer_idx],
            node_update_matrix[layer_idx],
        )
    charges = jnp.dot(hidden, latent_ionic_readout, preferred_element_type=jnp.float32) * occupied[
        :, None
    ].astype(jnp.float32)
    total_atoms = slab_rows * n_slab
    overall_mode_number = reciprocal_lattice_modes.shape[1] * mode_batch_number
    prefactor_scale = 4.0 / math.sqrt(total_atoms * overall_mode_number)
    charges_per_slab = lax.all_gather(charges, "kgrp", axis=0, tiled=True)
    mode_ewald_coefficient = ewald_screening_coef(reciprocal_lattice_modes, prefactor_scale)
    structure_arguments = maximum_entry(layer_cell_locations.T, reciprocal_lattice_modes)
    cosine_terms = jnp.cos(structure_arguments)
    sine_terms = jnp.sin(structure_arguments)
    real_component = maximum_entry(cosine_terms.T, charges_per_slab)
    imaginary_component = maximum_entry(sine_terms.T, charges_per_slab)
    real_component, imaginary_component = lax.psum((real_component, imaginary_component), "slab")
    potential_part, forces_part = respond(
        cosine_terms,
        sine_terms,
        charges_per_slab,
        real_component,
        imaginary_component,
        reciprocal_lattice_modes,
        mode_ewald_coefficient,
    )
    potential, forces = (
        lax.psum_scatter(potential_part, "kgrp", scatter_dimension=1, tiled=True),
        lax.psum_scatter(forces_part, "kgrp", scatter_dimension=1, tiled=True),
    )
    return (potential, forces)


def solution(mesh):
    return jax.shard_map(
        shards,
        mesh=mesh,
        in_specs=(
            P(("slab", "kgrp"), None),
            P(None, ("slab", "kgrp")),
            P(("slab", "kgrp"), None),
            P(("slab", "kgrp")),
            P(),
            P(None, "kgrp"),
            P(),
            P(),
            P(),
            P(),
        ),
        out_specs=(P(None, ("slab", "kgrp")), P(None, ("slab", "kgrp"))),
        check_vma=False,
    )
```

profile of v0, /device:TPU:1, one launch (start us, length us, event | category | flops | bytes accessed | tf_op | source)
XLA Modules:
  0.0 819.0 jit_solution(6602674491154741182)
XLA Ops:
  7.2 37.6 %all_gather.12 = f32[3,1024]{1,0:T(4,128)S(1)} all-gather(f32[3,128]{1,0:T(4,128)} %param.13), channel_id=1, replica_groups=mesh['slab'=32,'kgrp'=8] {'kgrp'}, dimensions={1}, use_global_device_ids=true | all-gather | bytes 13824 | tf_op jit(solution)/shard_map/all_gather | solution.py:97
  44.9 5.9 collective-permute-start.1
  51.4 0.9 convolution_convert_fusion.1
  52.3 38.6 %all_gather.13 = bf16[1024,128]{1,0:T(8,128)(2,1)S(1)} all-gather(bf16[128,128]{1,0:T(8,128)(2,1)S(1)} %convolution_convert_fusion.1), channel_id=1, replica_groups=mesh['slab'=32,'kgrp'=8] {'kgrp'}, dimensions={0}, use_global_device_ids=true | all-gather | bytes 294912 | tf_op jit(solution)/shard_map/all_gather | solution.py:112
  90.9 6.2 collective-permute-start.3
  99.1 0.8 copy.27
  100.0 1.2 dynamic_slice.3
  101.3 1.3 gather_fusion
  103.0 50.7 %gather_fusion.1 = pred[8192]{0:T(1024)(128)(4,1)S(1)} fusion(pred[3072]{0:T(1024)(128)(4,1)S(1)} %lt.111, s32[8192]{0:T(1024)S(1)} %broadcast_clamp_fusion.1), kind=kCustom, calls=%fused_computation.3 | custom fusion | bytes 49152 | tf_op jit(solution)/shard_map/jit(_take)/gather | solution.py:104
  155.3 27.8 %gather_fusion.2 = f32[8192,3]{1,0:T(8,128)} fusion(f32[3,3072]{0,1:T(8,128)S(1)} %copy.32, s32[8192]{0:T(1024)S(1)} %broadcast_clamp_fusion.1), kind=kCustom, calls=%fused_computation.4 | custom fusion | bytes 229376 | tf_op jit(solution)/shard_map/jit(_take)/gather | solution.py:99
  183.1 3.7 copy.33
  187.0 24.0 %gather_fusion.3 = bf16[8192,128]{1,0:T(8,128)(2,1)S(1)} fusion(bf16[3072,128]{1,0:T(8,128)(2,1)S(1)} %pad_maximum_fusion, s32[8192]{0:T(1024)S(1)} %broadcast_clamp_fusion), kind=kCustom, calls=%fused_computation.clone | custom fusion | bytes 4227072 | tf_op jit(solution)/shard_map/jit(_take)/gather | solution.py:116
  211.1 14.4 %select_reduce_fusion.1 = f32[128,128]{1,0:T(8,128)S(1)} fusion(bf16[128,64,128]{2,1,0:T(8,128)(2,1)S(1)} %bitcast.53, pred[128,64]{0,1:T(8,128)(4,1)S(1)} %compare_and_fusion.1, pred[128,64]{0,1:T(8,128)(4,1)S(1)} %copy.30, f32[128,64]{0,1:T(8,128)S(1)} %fusion.32, f32[8]{0:T(128)S(1)} %convert_multiply_fusion, f32[2,8,128]{2,1,0:T(8,128)S(1)} %copy-done.12), kind=kOutput, calls=%fused_computation.10 | convolution fusion | flops 106086400 | bytes 2216448 | tf_op jit(solution)/shard_map/bae,bc->aec/dot_general | solution.py:36
  225.8 38.4 %all_gather.14 = bf16[1024,128]{1,0:T(8,128)(2,1)S(1)} all-gather(bf16[128,128]{1,0:T(8,128)(2,1)S(1)} %convolution_convert_fusion), channel_id=1, replica_groups=mesh['slab'=32,'kgrp'=8] {'kgrp'}, dimensions={0}, use_global_device_ids=true | all-gather | bytes 294912 | tf_op jit(solution)/shard_map/all_gather | solution.py:112
  264.2 6.2 collective-permute-start.5
  270.3 0.9 collective-permute-start.4
  271.2 22.1 %fusion.61 = (f32[1024,1024]{1,0:T(8,128)}, f32[1024,1024]{1,0:T(8,128)}) fusion(f32[3,1024]{1,0:T(4,128)S(1)} %all_gather.12, f32[3,1024]{1,0:T(4,128)S(1)} %copy-done.6), kind=kOutput, calls=%fused_computation.103 | convolution fusion | flops 37748736 | bytes 8413184 | tf_op jit(solution)/shard_map/dot_general | solution.py:44
  293.4 24.0 %gather_fusion.4 = bf16[8192,128]{1,0:T(8,128)(2,1)S(1)} fusion(bf16[3072,128]{1,0:T(8,128)(2,1)S(1)} %pad_maximum_fusion.1, s32[8192]{0:T(1024)S(1)} %broadcast_clamp_fusion), kind=kCustom, calls=%fused_computation.1.clone | custom fusion | bytes 4227072 | tf_op jit(solution)/shard_map/jit(_take)/gather | solution.py:116
  317.4 14.4 %select_reduce_fusion = f32[128,128]{1,0:T(8,128)S(1)} fusion(bf16[128,64,128]{2,1,0:T(8,128)(2,1)S(1)} %bitcast.52, pred[128,64]{0,1:T(8,128)(4,1)S(1)} %compare_and_fusion.1, pred[128,64]{0,1:T(8,128)(4,1)S(1)} %copy.30, f32[128,64]{0,1:T(8,128)S(1)} %fusion.32, f32[8]{0:T(128)S(1)} %convert_multiply_fusion, f32[2,8,128]{2,1,0:T(8,128)S(1)} %copy-done.12), kind=kOutput, calls=%fused_computation.9 | convolution fusion | flops 106086400 | bytes 2216448 | tf_op jit(solution)/shard_map/bae,bc->aec/dot_general | solution.py:36
  332.1 38.2 %all_gather.15 = f32[1024,16]{0,1:T(8,128)S(1)} all-gather(f32[128,16]{0,1:T(8,128)S(1)} %convolution_multiply_fusion), channel_id=1, replica_groups=mesh['slab'=32,'kgrp'=8] {'kgrp'}, dimensions={0}, use_global_device_ids=true | all-gather | bytes 73728 | tf_op jit(solution)/shard_map/all_gather | solution.py:128
  370.3 5.1 fusion.63
  375.3 2.9 fusion.62
  378.3 258.1 %all-reduce.3.cloned.1.call-done = (f32[1024,16]{0,1:T(8,128)}, f32[1024,16]{0,1:T(8,128)}) async-done(((f32[1024,16]{0,1:T(8,128)}, f32[1024,16]{0,1:T(8,128)}), (f32[1024,16]{0,1:T(8,128)}, f32[1024,16]{0,1:T(8,128)})) %all-reduce.3.cloned.1.call-update) | async-done | bytes 131088 | tf_op jit(solution)/shard_map/psum | solution.py:135
  636.4 5.7 fusion.25
  642.2 3.5 fusion.23
  645.7 3.5 fusion.20
  649.2 4.4 fusion.7
  653.6 1.1 copy.38
  654.7 6.3 convolution_add_fusion
  661.0 76.0 %reduce-scatter.7.cloned.1.call-done = f32[128,3]{1,0:T(8,128)} async-done(((f32[1024,3]{1,0:T(8,128)}), f32[128,3]{1,0:T(8,128)}) %reduce-scatter.7.cloned.1.call-update) | async-done | bytes 1552
  737.0 1.5 copy.39
  738.5 74.0 %reduce-scatter.5.cloned.1.call-done = f32[16,128]{1,0:T(8,128)} async-done(((f32[16,1024]{1,0:T(8,128)}), f32[16,128]{1,0:T(8,128)}) %reduce-scatter.5.cloned.1.call-update) | async-done | bytes 8208 | tf_op jit(solution)/shard_map/reduce_scatter | solution.py:146
  (70 shorter events, 5.6 us)
Async XLA Ops:
  7.2 324.6 %copy-start = (bf16[128,16]{0,1:T(8,128)(2,1)S(1)}, bf16[128,16]{0,1:T(8,128)(2,1)}, u32[]{:S(2)}) copy-start(bf16[128,16]{0,1:T(8,128)(2,1)} %param.21) | copy-start | bytes 12292
  7.2 629.2 %all-reduce.3.cloned.1.call-start = ((), (), s32[]{:S(2)}) async-start(), calls=%async_computation.4 | async-start | bytes 262144 | tf_op jit(solution)/shard_map/psum | solution.py:135
  44.9 109.9 %collective-permute-start.1 = (f32[3,1024]{1,0:T(4,128)S(1)}, f32[3,1024]{1,0:T(4,128)S(1)}, u32[]{:S(2)}, u32[]{:S(2)}) collective-permute-start(f32[3,1024]{1,0:T(4,128)S(1)} %all_gather.12), channel_id=1, source_target_pairs={{8,0},{16,8},{24,16},{32,24},{40,32},{48,40},{56,48},{64,56},{72,6... | collective-permute-start | bytes 36872 | tf_op jit(solution)/shard_map/ppermute | solution.py:18
  50.8 104.0 %collective-permute-start = (f32[3,1024]{1,0:T(4,128)S(1)}, f32[3,1024]{1,0:T(4,128)S(1)}, u32[]{:S(2)}, u32[]{:S(2)}) collective-permute-start(f32[3,1024]{1,0:T(4,128)S(1)} %all_gather.12), channel_id=1, source_target_pairs={{0,8},{8,16},{16,24},{24,32},{32,40},{40,48},{48,56},{56,64},{64,7... | collective-permute-start | bytes 36872 | tf_op jit(solution)/shard_map/ppermute | solution.py:16
  90.9 96.0 %collective-permute-start.3 = (bf16[1024,128]{1,0:T(8,128)(2,1)S(1)}, bf16[1024,128]{1,0:T(8,128)(2,1)S(1)}, u32[]{:S(2)}, u32[]{:S(2)}) collective-permute-start(bf16[1024,128]{1,0:T(8,128)(2,1)S(1)} %all_gather.13), channel_id=1, source_target_pairs={{8,0},{16,8},{24,16},{32,24},{40,32},{48,40},{56,48},{64,56},{72,6... | collective-permute-start | bytes 786440 | tf_op jit(solution)/shard_map/ppermute | solution.py:18
  97.1 89.8 %collective-permute-start.2 = (bf16[1024,128]{1,0:T(8,128)(2,1)S(1)}, bf16[1024,128]{1,0:T(8,128)(2,1)S(1)}, u32[]{:S(2)}, u32[]{:S(2)}) collective-permute-start(bf16[1024,128]{1,0:T(8,128)(2,1)S(1)} %all_gather.13), channel_id=1, source_target_pairs={{0,8},{8,16},{16,24},{24,32},{32,40},{40,48},{48,56},{56,64},{64,7... | collective-permute-start | bytes 786440 | tf_op jit(solution)/shard_map/ppermute | solution.py:16
  103.0 51.5 %copy-start.10 = (s32[128]{0:T(128)S(1)}, s32[128]{0:T(128)}, u32[]{:S(2)}) copy-start(s32[128]{0:T(128)} %param.15) | copy-start | bytes 1540
  153.7 33.2 %copy-start.9 = (f32[3,128]{1,0:T(4,128)S(1)}, f32[3,128]{1,0:T(4,128)}, u32[]{:S(2)}) copy-start(f32[3,128]{1,0:T(4,128)} %param.13) | copy-start | bytes 4612
  187.0 24.0 %copy-start.12 = (f32[2,8,128]{2,1,0:T(8,128)S(1)}, f32[2,8,128]{2,1,0:T(8,128)}, u32[]{:S(2)}) copy-start(f32[2,8,128]{2,1,0:T(8,128)} %param.20) | copy-start | bytes 24580
  211.1 14.4 %copy-start.8 = (bf16[128,128]{1,0:T(8,128)(2,1)S(1)}, bf16[128,128]{1,0:T(8,128)(2,1)}, u32[]{:S(2)}) copy-start(bf16[128,128]{1,0:T(8,128)(2,1)} %param.12) | copy-start | bytes 98308
  211.1 14.4 %copy-start.11 = (bf16[2,128,128]{2,1,0:T(8,128)(2,1)S(1)}, bf16[2,128,128]{2,1,0:T(8,128)(2,1)}, u32[]{:S(2)}) copy-start(bf16[2,128,128]{2,1,0:T(8,128)(2,1)} %param.19) | copy-start | bytes 196612
  211.1 14.6 %copy-start.7 = (bf16[2,128,128]{2,1,0:T(8,128)(2,1)S(1)}, bf16[2,128,128]{2,1,0:T(8,128)(2,1)}, u32[]{:S(2)}) copy-start(bf16[2,128,128]{2,1,0:T(8,128)(2,1)} %param.18) | copy-start | bytes 196612
  211.1 60.1 %copy-start.6 = (f32[3,1024]{1,0:T(4,128)S(1)}, f32[3,1024]{1,0:T(4,128)}, u32[]{:S(2)}) copy-start(f32[3,1024]{1,0:T(4,128)} %param.17) | copy-start | bytes 36868
  264.2 29.1 %collective-permute-start.5 = (bf16[1024,128]{1,0:T(8,128)(2,1)S(1)}, bf16[1024,128]{1,0:T(8,128)(2,1)S(1)}, u32[]{:S(2)}, u32[]{:S(2)}) collective-permute-start(bf16[1024,128]{1,0:T(8,128)(2,1)S(1)} %all_gather.14), channel_id=1, source_target_pairs={{8,0},{16,8},{24,16},{32,24},{40,32},{48,40},{56,48},{64,56},{72,6... | collective-permute-start | bytes 786440 | tf_op jit(solution)/shard_map/ppermute | solution.py:18
  270.3 23.0 %collective-permute-start.4 = (bf16[1024,128]{1,0:T(8,128)(2,1)S(1)}, bf16[1024,128]{1,0:T(8,128)(2,1)S(1)}, u32[]{:S(2)}, u32[]{:S(2)}) collective-permute-start(bf16[1024,128]{1,0:T(8,128)(2,1)S(1)} %all_gather.14), channel_id=1, source_target_pairs={{0,8},{8,16},{16,24},{24,32},{32,40},{40,48},{48,56},{56,64},{64,7... | collective-permute-start | bytes 786440 | tf_op jit(solution)/shard_map/ppermute | solution.py:16
  332.1 43.3 %copy-start.2 = (f32[1024,1024]{1,0:T(8,128)S(1)}, f32[1024,1024]{1,0:T(8,128)}, u32[]{:S(2)}) copy-start(f32[1024,1024]{1,0:T(8,128)} %get-tuple-element.10) | copy-start | bytes 12582916
  378.3 358.7 %reduce-scatter.7.cloned.1.call-start = ((), (), s32[]{:S(2)}) async-start(), calls=%async_computation.3 | async-start | bytes 589824
  636.4 5.8 copy-start.5
  636.4 9.3 %copy-start.4 = (f32[1024,16]{0,1:T(8,128)S(1)}, f32[1024,16]{0,1:T(8,128)}, u32[]{:S(2)}) copy-start(f32[1024,16]{0,1:T(8,128)} %get-tuple-element.4) | copy-start | bytes 196612
  642.2 7.0 copy-start.1
  642.2 7.0 copy-start.3
  654.6 157.8 %reduce-scatter.5.cloned.1.call-start = ((), (), s32[]{:S(2)}) async-start(), calls=%async_computation.2 | async-start | bytes 73728 | tf_op jit(solution)/shard_map/reduce_scatter | solution.py:146
Sparse Core Ops, SparseCore 0:
  378.4 257.9 all-reduce.2
  654.8 82.1 reduce-scatter.6
  741.2 71.1 reduce-scatter.4
where the time goes:
time: 821 us; the launch traced here: 819 us
  waiting for transfers between devices  408 us (50%)
  blocking collectives  153 us (19%)
  local copies, waits for them, and re-layouts  137 us (17%)
  matrix products  83.6 us (10%)
  starting transfers between devices  20.4 us (2%)
  between operations  14.2 us (2%)
    psum x1, waiting for transfers between devices, shards(): lax.psum((real_component, imaginary_component), 'slab')  258 us
    all_gather x2, blocking collectives, shards(): slab_messages = lax.all_gather(message_rows, 'kgrp', axis=0, tiled=True)  77 us
    unnamed x4, waiting for transfers between devices  76 us
    reduce_scatter x1, waiting for transfers between devices, shards(): lax.psum_scatter(potential_part, 'kgrp', scatter_dimension=1, tiled=True)  74 us
    dot_general x8, matrix products, maximum_entry(): jnp.dot(left, right, precision=lax.Precision.HIGHEST, preferred_element_t...  53.4 us
    gather x2, local copies, waits for them, and re-layouts, shards(): jnp.take(occupied_ext, adjacent_atom_slots)  50.8 us
    gather x2, local copies, waits for them, and re-layouts, shards(): jnp.take(ext_messages, adjacent_atom_slots, axis=0)  48.1 us
    all_gather x1, blocking collectives, shards(): charges_per_slab = lax.all_gather(charges, 'kgrp', axis=0, tiled=True)  38.2 us
  transfers between devices with their start and end apart: 9, of which 3 were waited for; matrix products, arithmetic and copies ran while one was open for 15% of the time, Pallas kernels for 0%

commit v1 on v0

v1 whole, which is shorter than its diff:
```python
import math

import jax
import jax.numpy as jnp
from jax import lax
from jax.experimental import pallas as pl
from jax.experimental.pallas import tpu as pltpu
from jax.sharding import PartitionSpec as P

AXES = ("slab", "kgrp")
F32 = jnp.float32
BF16 = jnp.bfloat16
MIB = 1 << 20

ROWS = 128
PAYLOAD = 144

CENTRE = 3.04
SINC = (4.53143365e-01, -1.10011030e-01, 6.70800349e-03, -1.85302418e-04, 2.92602795e-06, -2.98676509e-08)
TWOCOS = (-5.04597246e-01, -5.81178942e-01, 7.05473141e-02, -2.86778430e-03, 5.94149034e-05, -7.50432042e-07, 6.38391477e-09)
SINTURN = (6.2831853, -41.34170041, 81.60513139, -76.70301535, 42.02592698, -14.89984666, 3.2381375)
COSTURN = (0.99999999, -19.7392045, 64.93911746, -85.45013953, 60.16763095, -25.96759925, 6.52865816)


def horner(coefficients, x):
    value = coefficients[-1] * x + coefficients[-2]
    for c in coefficients[-3::-1]:
        value = value * x + c
    return value


def split(x, parts):
    pieces = []
    for i in range(parts):
        piece = x.astype(BF16)
        pieces.append(piece)
        if i + 1 < parts:
            x = x - piece.astype(F32)
    return pieces


def nt(a, b):
    return lax.dot_general(a, b, (((1,), (1,)), ((), ())), preferred_element_type=F32)


def nn(a, b):
    return jnp.dot(a, b, preferred_element_type=F32)


def call(body, out_shape, *operands, scalars=(), name, flops=0, limit=32, **kw):
    specs = [pl.BlockSpec(memory_space=pltpu.SMEM)] * len(scalars)
    in_specs = specs + kw.pop("in_specs", [pl.BlockSpec(memory_space=pltpu.VMEM)] * len(operands))
    return pl.pallas_call(
        body,
        out_shape=out_shape,
        in_specs=in_specs,
        name=name,
        cost_estimate=pl.CostEstimate(flops=flops, bytes_accessed=MIB, transcendentals=0),
        compiler_params=pltpu.CompilerParams(vmem_limit_bytes=limit * MIB),
        **kw,
    )(*scalars, *operands)


def pack_body(desc_ref, loc_ref, out_ref):
    out_ref[0:ROWS, :] = desc_ref[...]
    hi, mid, lo = [p.astype(F32) for p in split(loc_ref[...], 3)]
    tail = jnp.concatenate([hi, mid, lo, jnp.zeros((7, ROWS), F32)], axis=0)
    out_ref[ROWS:PAYLOAD, :] = tail.astype(BF16)


def coordinates(payload):
    tail = payload[ROWS:PAYLOAD, :].astype(F32)
    return (tail[0:3] + tail[3:6]) + tail[6:9]


def count_body(scal_ref, slots_ref, tally_ref, cnt_ref):
    y, zh, odd = scal_ref[0], scal_ref[1], scal_ref[2]
    f_prev, f_own, f_next, base = scal_ref[3], scal_ref[4], scal_ref[5], scal_ref[6]
    slots = slots_ref[...]
    shape = slots.shape
    lane = lax.broadcasted_iota(jnp.int32, shape, 1)
    row = lax.broadcasted_iota(jnp.int32, shape, 0)
    local = lane >> 6
    atom = row * 8 + local + base
    region = slots >> 10
    within = slots & 1023
    filled = jnp.where(region == 0, f_prev, jnp.where(region == 1, f_own, f_next))
    usable = ((lane & 63) < tally_ref[...]) & (within < filled) & (atom < f_own)
    place = jnp.where(region == 1, 0, jnp.where(region == 2 * odd, 1, 2))
    kblock = within >> 7
    inner = ((((kblock >> 1) - y) & 3) << 1) | ((kblock & 1) ^ zh)
    target = jnp.where(usable, (place * 8 + inner) * 8 + local, -1)
    low = slots & 127
    iota_p = lax.broadcasted_iota(jnp.int32, (192, 512), 0)
    iota_l = lax.broadcasted_iota(jnp.int32, (128, 512), 0)
    for i in range(16):
        p = jnp.where(iota_p == target[i : i + 1], 1.0, 0.0).astype(BF16)
        l = jnp.where(iota_l == low[i : i + 1], 1.0, 0.0).astype(BF16)
        cnt_ref[:, 8 * i : 8 * i + 8, :] = nt(p, l).reshape(24, 8, 128)


def update(gathered, hidden, self_weight):
    drive = gathered * 0.125 + nn(hidden, self_weight)
    return (hidden.astype(F32) + drive * jax.nn.sigmoid(drive)).astype(BF16)


def mix(acc, mixing):
    total = acc[0:ROWS] * mixing[0:1]
    for n in range(1, 8):
        total = total + acc[n * ROWS : (n + 1) * ROWS] * mixing[n : n + 1]
    return total


def first_body(shift_ref, y0, y1, y2, y3, c0, c1, c2, c3, cnt_ref, here_ref, edge_ref, node_ref, mixing_ref, g_ref, hidden_ref, message_ref, m_s, x_s, acc_s):
    step = pl.program_id(0)

    @pl.when(step == 0)
    def _():
        for b in range(24):
            j, z = (b % 8) // 2, b % 2
            ref = (y0, y1, y2, y3)[j] if b < 16 else (c0, c1, c2, c3)[j]
            i = (b // 8) * 2 + z if b < 16 else z
            m_s[b // 4, (b % 4) * ROWS : (b % 4 + 1) * ROWS, :] = nn(ref[i, 0:ROWS, :], edge_ref[0]).astype(BF16)
            xyz = coordinates(ref[i])
            x_s[b, 0:1, :] = xyz[0:1] + shift_ref[b // 8]
            x_s[b, 1:3, :] = xyz[1:3]
        acc_s[...] = jnp.zeros_like(acc_s)

    for q in range(4):
        src = x_s[step * 4 + q]
        for r in range(0, ROWS, 64):
            here = here_ref[r : r + 64, :]
            dx = src[0:1] - here[:, 0:1]
            dy = src[1:2] - here[:, 1:2]
            dz = src[2:3] - here[:, 2:3]
            v = dx * dx + dy * dy + dz * dz + (0.04 - CENTRE)
            cur = cnt_ref[q, r : r + 64, :] * horner(SINC, v)
            turn = horner(TWOCOS, v)
            prev = None
            for n in range(8):
                g_ref[n * ROWS + r : n * ROWS + r + 64, q * 128 : (q + 1) * 128] = cur.astype(BF16)
                nxt = turn * cur if prev is None else turn * cur - prev
                prev, cur = cur, nxt
    acc_s[...] += nn(g_ref[...], m_s[step])

    @pl.when(step == 5)
    def _():
        hidden = update(mix(acc_s[...], mixing_ref[0]), y0[0, 0:ROWS, :], node_ref[0])
        hidden_ref[...] = hidden
        message_ref[...] = nn(hidden, edge_ref[1]).astype(BF16)


def second_body(scal_ref, y0, y1, y2, y3, c0, c1, c2, c3, g_ref, hidden_ref, node_ref, mixing_ref, readout_ref, charge_ref, m_s, acc_s):
    step = pl.program_id(0)

    @pl.when(step == 0)
    def _():
        for b in range(24):
            j, z = (b % 8) // 2, b % 2
            ref = (y0, y1, y2, y3)[j] if b < 16 else (c0, c1, c2, c3)[j]
            i = (b // 8) * 2 + z if b < 16 else z
            m_s[b // 4, (b % 4) * ROWS : (b % 4 + 1) * ROWS, :] = ref[i]
        acc_s[...] = jnp.zeros_like(acc_s)

    acc_s[...] += nn(g_ref[...], m_s[step])

    @pl.when(step == 5)
    def _():
        hidden = update(mix(acc_s[...], mixing_ref[1]), hidden_ref[...], node_ref[1])
        charges = nt(readout_ref[...], hidden)
        atom = lax.broadcasted_iota(jnp.int32, charges.shape, 1) + scal_ref[6]
        charge_ref[...] = jnp.where(atom < scal_ref[4], charges, 0.0)


def phase_body(y0, y1, y2, y3, modes_ref, wave_ref):
    for b in range(8):
        xyz = coordinates((y0, y1, y2, y3)[b // 2][b % 2])
        for r in range(0, 1024, 64):
            k = modes_ref[r : r + 64, :]
            turns = k[:, 0:1] * xyz[0:1] + k[:, 1:2] * xyz[1:2] + k[:, 2:3] * xyz[2:3]
            rest = turns - jnp.round(turns)
            square = rest * rest
            wave_ref[r : r + 64, b * 128 : (b + 1) * 128] = horner(COSTURN, square).astype(BF16)
            wave_ref[1024 + r : 1024 + r + 64, b * 128 : (b + 1) * 128] = (rest * horner(SINTURN, square)).astype(BF16)


def structure_body(place_ref, wave_ref, charge_ref, out_ref, q_ref):
    charges = jnp.concatenate([charge_ref[place_ref[b]] for b in range(8)], axis=1)
    q_ref[...] = charges
    pieces = jnp.concatenate(split(charges, 3), axis=0)
    for i in range(2):
        for r in range(0, 1024, 128):
            s = nt(wave_ref[i * 1024 + r : i * 1024 + r + 128, :], pieces)
            s = s[:, 0:16] + s[:, 16:32] + s[:, 32:48]
            out_ref[i * 16 : (i + 1) * 16, r : r + 128] = s.T


def respond_body(place_ref, scale_ref, wave_ref, sum_ref, q_ref, modes_ref, out_ref):
    k = modes_ref[...]
    square = k[0:1] * k[0:1] + k[1:2] * k[1:2] + k[2:3] * k[2:3]
    weight = scale_ref[0] * jnp.exp(square * -0.125) / (square + 1.0)
    real = sum_ref[0:16, :] * weight
    imag = sum_ref[16:32, :] * weight
    left = [real] + [imag * k[j : j + 1] for j in range(3)]
    right = [imag] + [real * -k[j : j + 1] for j in range(3)]
    both = jnp.concatenate([jnp.concatenate(left, axis=0), jnp.concatenate(right, axis=0)], axis=1)
    out = nn(jnp.concatenate(split(both, 2), axis=0), wave_ref[...])
    out = out[0:64] + out[64:128]
    force = [-jnp.sum(out[16 * j + 16 : 16 * j + 32] * q_ref[...], axis=0, keepdims=True) for j in range(3)]
    full = jnp.concatenate([out[0:16]] + force + [jnp.zeros((5, 1024), F32)], axis=0)
    for b in range(8):
        out_ref[place_ref[b]] = full[:, b * 128 : (b + 1) * 128]


def pairs(n_slab, target):
    return [(s * 8 + k, (target(s, k)[0] % n_slab) * 8 + target(s, k)[1]) for s in range(n_slab) for k in range(8)]


def move(x, target):
    return lax.ppermute(x, AXES, pairs(lax.axis_size("slab"), target))


def over_chip(s):
    return s + 1 if s % 2 else s - 1


def surroundings(block):
    near = move(block, lambda s, k: (over_chip(s), k))
    half = move(block, lambda s, k: (s, k ^ 1))
    both = move(block, lambda s, k: (over_chip(s), k ^ 1))
    stack = jnp.stack([block, half, near, both])
    ys = [stack]
    for j in range(1, 4):
        ys.append(move(stack, lambda s, k: (s, (k - 2 * j) % 8)))
    cs = [move(y[0:2], lambda s, k: (s ^ 1, k)) for y in ys]
    return ys + cs


def shards(
    atom_descriptors,
    atom_locations,
    adjacent_atom_slots,
    neighbour_tally,
    filled_slot_tallies,
    reciprocal_lattice_modes,
    edge_update_matrix,
    node_update_matrix,
    distance_basis_mixing,
    latent_ionic_readout,
):
    n_slab = lax.axis_size("slab")
    slab = lax.axis_index("slab")
    group = lax.axis_index("kgrp")
    odd = slab % 2
    y, zh = group // 2, group % 2
    filled = jnp.take(filled_slot_tallies, (slab + jnp.arange(3) - 1) % n_slab)
    scal = jnp.concatenate([jnp.stack([y, zh, odd]), filled, jnp.stack([group * ROWS, 0])]).astype(jnp.int32)
    low_edge = jnp.where(slab == 0, -float(n_slab), 0.0)
    high_edge = jnp.where(slab == n_slab - 1, float(n_slab), 0.0)
    shift = jnp.stack([0.0, jnp.where(odd == 1, high_edge, low_edge), jnp.where(odd == 1, low_edge, high_edge)]).astype(F32)
    spots = jnp.arange(8, dtype=jnp.int32)
    place = (((y + spots // 2) % 4) * 2 + ((spots % 2) ^ zh)).astype(jnp.int32)

    block = call(pack_body, jax.ShapeDtypeStruct((PAYLOAD, ROWS), BF16), atom_descriptors, atom_locations, name="pack")
    first = surroundings(block)
    counts = call(
        count_body,
        jax.ShapeDtypeStruct((24, ROWS, 128), F32),
        adjacent_atom_slots.reshape(16, 512),
        jnp.broadcast_to(neighbour_tally[:, None], (ROWS, 64)).reshape(16, 512),
        scalars=(scal,),
        name="counts",
        flops=10**9,
    )
    whole = lambda *shape: pl.BlockSpec(shape, lambda i: (0,) * len(shape))
    near_specs = lambda rows: [whole(4, rows, ROWS)] * 4 + [whole(2, rows, ROWS)] * 4
    basis, hidden, messages = call(
        first_body,
        (
            jax.ShapeDtypeStruct((8 * ROWS, 24 * ROWS), BF16),
            jax.ShapeDtypeStruct((ROWS, 128), BF16),
            jax.ShapeDtypeStruct((ROWS, 128), BF16),
        ),
        *first,
        counts,
        atom_locations.T,
        edge_update_matrix,
        node_update_matrix,
        distance_basis_mixing,
        scalars=(shift,),
        name="first_layer",
        flops=10**9,
        grid=(6,),
        in_specs=near_specs(PAYLOAD)
        + [pl.BlockSpec((4, ROWS, 128), lambda i: (i, 0, 0)), whole(ROWS, 3), whole(2, 128, 128), whole(2, 128, 128), whole(2, 8, 128)],
        out_specs=[pl.BlockSpec((8 * ROWS, 512), lambda i: (0, i)), whole(ROWS, 128), whole(ROWS, 128)],
        scratch_shapes=[pltpu.VMEM((6, 512, 128), BF16), pltpu.VMEM((24, 3, 128), F32), pltpu.VMEM((8 * ROWS, 128), F32)],
    )
    second = surroundings(messages)
    turns = reciprocal_lattice_modes.T * (0.5 / math.pi)
    waves = call(
        phase_body, jax.ShapeDtypeStruct((2048, 1024), BF16), *first[:4], turns, name="phases", flops=2 * 10**9
    )
    charges = call(
        second_body,
        jax.ShapeDtypeStruct((16, ROWS), F32),
        *second,
        basis,
        hidden,
        node_update_matrix,
        distance_basis_mixing,
        latent_ionic_readout.T,
        scalars=(scal,),
        name="second_layer",
        flops=10**9,
        grid=(6,),
        in_specs=near_specs(ROWS)
        + [pl.BlockSpec((8 * ROWS, 512), lambda i: (0, i)), whole(ROWS, 128), whole(2, 128, 128), whole(2, 8, 128), whole(16, 128)],
        out_specs=whole(16, ROWS),
        scratch_shapes=[pltpu.VMEM((6, 512, 128), BF16), pltpu.VMEM((8 * ROWS, 128), F32)],
    )
    slab_charges = lax.all_to_all(jnp.broadcast_to(charges[None], (8, 16, ROWS)), "kgrp", 0, 0)
    sums, q = call(
        structure_body,
        (jax.ShapeDtypeStruct((32, 1024), F32), jax.ShapeDtypeStruct((16, 1024), F32)),
        waves,
        slab_charges,
        scalars=(place,),
        name="structure",
        flops=10**8,
    )
    lower, upper = sums[:, :512], sums[:, 512:]
    is_odd = odd == 1
    part = jnp.where(is_odd, upper, lower) + move(jnp.where(is_odd, lower, upper), lambda s, k: (s ^ 1, k))
    part = part + sum(move(part, lambda s, k, m=m: (s ^ (2 * m), k)) for m in (1, 2, 3))
    part = part + sum(move(part, lambda s, k, m=m: (s + 8 * m, k)) for m in (1, 2, 3))
    other = move(part, lambda s, k: (s ^ 1, k))
    total = jnp.where(is_odd, jnp.concatenate([other, part], axis=1), jnp.concatenate([part, other], axis=1))
    scale = jnp.full((1,), 4.0 / math.sqrt(n_slab * 1024 * reciprocal_lattice_modes.shape[1] * 8), F32)
    partial = call(
        respond_body,
        jax.ShapeDtypeStruct((8, 24, ROWS), F32),
        waves,
        total,
        q,
        reciprocal_lattice_modes,
        scalars=(place, scale),
        name="respond",
        flops=10**8,
    )
    result = jnp.sum(lax.all_to_all(partial, "kgrp", 0, 0), axis=0)
    return result[:16], result[16:19]


def solution(mesh):
    return jax.shard_map(
        shards,
        mesh=mesh,
        in_specs=(
            P(("slab", "kgrp"), None),
            P(None, ("slab", "kgrp")),
            P(("slab", "kgrp"), None),
            P(("slab", "kgrp")),
            P(),
            P(None, "kgrp"),
            P(),
            P(),
            P(),
            P(),
        ),
        out_specs=(P(None, ("slab", "kgrp")), P(None, ("slab", "kgrp"))),
        check_vma=False,
    )
```

time: 821 us -> 133 us (0.16)
  waiting for transfers between devices: 408 us -> 16.8 us
  blocking collectives: 153 us -> 16 us
  local copies, waits for them, and re-layouts: 137 us -> 15.8 us
  matrix products: 83.6 us -> 0 us
  starting transfers between devices: 20.4 us -> 59.5 us
  Pallas kernels: 0 us -> 22.6 us
  between operations: 14.2 us -> 0.98 us
    psum x1 -> x0, waiting for transfers between devices: 258 us -> none  [shards(): lax.psum((real_component, imaginary_component), 'slab')]
    all_gather x4 -> x0, blocking collectives: 153 us -> none  [the longest x2 77 us: shards(): slab_messages = lax.all_gather(message_rows, 'kgrp', axis=0, tiled=True)]
    gather x7 -> x1, local copies, waits for them, and re-layouts: 132 us -> 0.64 us  [shards(): filled = jnp.take(filled_slot_tallies, (slab + jnp.arange(3) - 1) % n_slab)]
    dot_general x14 -> x0, matrix products: 83.6 us -> none  [the longest x8 53.4 us: maximum_entry(): jnp.dot(left, right, precision=lax.Precision.HIGHEST, preferred_element_t...]
    unnamed x4 -> x0, waiting for transfers between devices: 76 us -> none
    reduce_scatter x1 -> x0, waiting for transfers between devices: 74 us -> none  [shards(): lax.psum_scatter(potential_part, 'kgrp', scatter_dimension=1, tiled=True)]
    ppermute x6 -> x28, starting transfers between devices: 20.2 us -> 53.2 us  [move(): return lax.ppermute(x, AXES, pairs(lax.axis_size('slab'), target))]
    pallas_call x0 -> x7, Pallas kernels: none -> 22.6 us  [call(): pl.pallas_call(body, out_shape=out_shape, in_specs=in_specs, name=name, c...]
  transfers between devices with their start and end apart: 9 -> 29, of which waited for: 3 -> 13; matrix products, arithmetic and copies ran while one was open for 15% -> 2% of each run, Pallas kernels for 0% -> 6%
where the time goes in v1:
time: 133 us; the launch traced here: 132 us
  starting transfers between devices  59.5 us (45%)
  Pallas kernels  22.6 us (17%)
  waiting for transfers between devices  16.8 us (13%)
  blocking collectives  16 us (12%)
  local copies, waits for them, and re-layouts  15.8 us (12%)
    ppermute x28, starting transfers between devices, move(): return lax.ppermute(x, AXES, pairs(lax.axis_size('slab'), target))  53.2 us
    pallas_call x7, Pallas kernels, call(): pl.pallas_call(body, out_shape=out_shape, in_specs=in_specs, name=name, c...  22.6 us
    all_to_all x1, blocking collectives, shards(): result = jnp.sum(lax.all_to_all(partial, 'kgrp', 0, 0), axis=0)  16 us
    ppermute x28, waiting for transfers between devices, move(): return lax.ppermute(x, AXES, pairs(lax.axis_size('slab'), target))  15.4 us
    unnamed x26, local copies, waits for them, and re-layouts  12 us
    all_to_all x1, starting transfers between devices, shards(): lax.all_to_all(jnp.broadcast_to(charges[None], (8, 16, ROWS)), 'kgrp', 0, 0)  6.33 us
  transfers between devices with their start and end apart: 29, of which 13 were waited for; matrix products, arithmetic and copies ran while one was open for 2% of the time, Pallas kernels for 6%

profile of v1, /device:TPU:1, one launch (start us, length us, event | category | flops | bytes accessed | tf_op | source)
XLA Modules:
  0.0 132.0 jit_solution(7366383911375668742)
XLA Ops:
  2.1 7.8 %collective-permute-start = (bf16[144,128]{1,0:T(8,128)(2,1)S(1)}, bf16[144,128]{1,0:T(8,128)(2,1)S(1)}, u32[]{:S(2)}, u32[]{:S(2)}) collective-permute-start(bf16[144,128]{1,0:T(8,128)(2,1)S(1)} %pack.1), channel_id=1, source_target_pairs={{0,1},{1,0},{2,3},{3,2},{4,5},{5,4},{6,7},{7,6},{8,9},{9,8},{10,11... | collective-permute-start | bytes 110600 | tf_op jit(solution)/shard_map/ppermute | solution.py:220
  10.0 1.6 %collective-permute-start.1 = (bf16[144,128]{1,0:T(8,128)(2,1)S(1)}, bf16[144,128]{1,0:T(8,128)(2,1)S(1)}, u32[]{:S(2)}, u32[]{:S(2)}) collective-permute-start(bf16[144,128]{1,0:T(8,128)(2,1)S(1)} %pack.1), channel_id=1, source_target_pairs={{0,248},{1,249},{2,250},{3,251},{4,252},{5,253},{6,254},{7,255},{8... | collective-permute-start | bytes 110600 | tf_op jit(solution)/shard_map/ppermute | solution.py:220
  12.3 2.7 %collective-permute-done.1 = bf16[144,128]{1,0:T(8,128)(2,1)S(1)} collective-permute-done((bf16[144,128]{1,0:T(8,128)(2,1)S(1)}, bf16[144,128]{1,0:T(8,128)(2,1)S(1)}, u32[]{:S(2)}, u32[]{:S(2)}) %collective-permute-start.1) | collective-permute-done | bytes 36896 | tf_op jit(solution)/shard_map/ppermute | solution.py:220
  15.0 3.0 %collective-permute-done.2 = bf16[144,128]{1,0:T(8,128)(2,1)S(1)} collective-permute-done((bf16[144,128]{1,0:T(8,128)(2,1)S(1)}, bf16[144,128]{1,0:T(8,128)(2,1)S(1)}, u32[]{:S(2)}, u32[]{:S(2)}) %collective-permute-start.2) | collective-permute-done | bytes 36896 | tf_op jit(solution)/shard_map/ppermute | solution.py:220
  18.1 2.8 %collective-permute-start.3 = (bf16[4,144,128]{2,1,0:T(8,128)(2,1)S(1)}, bf16[4,144,128]{2,1,0:T(8,128)(2,1)S(1)}, u32[]{:S(2)}, u32[]{:S(2)}) collective-permute-start(bf16[4,144,128]{2,1,0:T(8,128)(2,1)S(1)} %pad_maximum_fusion.y0), channel_id=1, source_target_pairs={{0,6},{1,7},{2,0},{3,1},{4,2},{5,3},{6,4},{7,5},{8,14},{9,15},{10,... | collective-permute-start | bytes 442376 | tf_op jit(solution)/shard_map/ppermute | solution.py:220
  24.1 4.1 %collective-permute-start.6 = (bf16[2,144,128]{2,1,0:T(8,128)(2,1)S(1)}, bf16[2,144,128]{2,1,0:T(8,128)(2,1)S(1)}, u32[]{:S(2)}, u32[]{:S(2)}) collective-permute-start(bf16[2,144,128]{2,1,0:T(8,128)(2,1)S(1)} %pad_maximum_fusion.2), channel_id=1, source_target_pairs={{0,8},{1,9},{2,10},{3,11},{4,12},{5,13},{6,14},{7,15},{8,0},{9,1},... | collective-permute-start | bytes 221192 | tf_op jit(solution)/shard_map/ppermute | solution.py:220
  28.6 2.5 %collective-permute-start.8 = (bf16[2,144,128]{2,1,0:T(8,128)(2,1)S(1)}, bf16[2,144,128]{2,1,0:T(8,128)(2,1)S(1)}, u32[]{:S(2)}, u32[]{:S(2)}) collective-permute-start(bf16[2,144,128]{2,1,0:T(8,128)(2,1)S(1)} %slice.47), channel_id=1, source_target_pairs={{0,8},{1,9},{2,10},{3,11},{4,12},{5,13},{6,14},{7,15},{8,0},{9,1},... | collective-permute-start | bytes 221192 | tf_op jit(solution)/shard_map/ppermute | solution.py:220
  31.1 1.5 %collective-permute-start.9 = (bf16[2,144,128]{2,1,0:T(8,128)(2,1)S(1)}, bf16[2,144,128]{2,1,0:T(8,128)(2,1)S(1)}, u32[]{:S(2)}, u32[]{:S(2)}) collective-permute-start(bf16[2,144,128]{2,1,0:T(8,128)(2,1)S(1)} %slice.48), channel_id=1, source_target_pairs={{0,8},{1,9},{2,10},{3,11},{4,12},{5,13},{6,14},{7,15},{8,0},{9,1},... | collective-permute-start | bytes 221192 | tf_op jit(solution)/shard_map/ppermute | solution.py:220
  32.7 1.7 %counts.1.cnt_ref = f32[24,128,128]{2,1,0:T(8,128)S(1)} custom-call(s32[8]{0:T(128)S(1)} %concatenate.11.scal_ref, s32[16,512]{1,0:T(8,128)S(1)} %reshape.70.slots_ref, s32[16,512]{1,0:T(8,128)S(1)} %broadcast_in_dim.20.tally_ref), custom_call_target="tpu_custom_call" | custom-call | flops 1000000000 | bytes 1048576 | tf_op jit(solution)/shard_map/counts/pallas_call | solution.py:53
  34.5 7.8 %first_layer.1 = (bf16[1024,3072]{1,0:T(8,128)(2,1)S(1)}, bf16[128,128]{1,0:T(8,128)(2,1)S(1)}, bf16[128,128]{1,0:T(8,128)(2,1)S(1)}) custom-call(f32[3]{0:T(128)S(1)} %pad_maximum_fusion.4.shift_ref, bf16[4,144,128]{2,1,0:T(8,128)(2,1)S(1)} %pad_maximum_fusion.y0, bf16[4,144,128]{2,1,0:T(8,128)(2,1)S(1)} %collective-permute-done.3.y1, ...), custom_call_target="tpu_custom_call" | custom-call | flops 1000000000 | bytes 1048576 | tf_op jit(solution)/shard_map/first_layer/pallas_call | solution.py:53
  42.3 2.6 %copy-done.3 = bf16[1024,3072]{1,0:T(8,128)(2,1)} copy-done((bf16[1024,3072]{1,0:T(8,128)(2,1)}, bf16[1024,3072]{1,0:T(8,128)(2,1)S(1)}, u32[]{:S(2)}) %copy-start.3) | copy-done | bytes 6291480
  46.4 4.4 %collective-permute-start.12 = (bf16[128,128]{1,0:T(8,128)(2,1)S(1)}, bf16[128,128]{1,0:T(8,128)(2,1)S(1)}, u32[]{:S(2)}, u32[]{:S(2)}) collective-permute-start(bf16[128,128]{1,0:T(8,128)(2,1)S(1)} %get-tuple-element.7), channel_id=1, source_target_pairs={{0,249},{1,248},{2,251},{3,250},{4,253},{5,252},{6,255},{7,254},{8... | collective-permute-start | bytes 98312 | tf_op jit(solution)/shard_map/ppermute | solution.py:220
  50.9 1.6 %collective-permute-done.10 = bf16[128,128]{1,0:T(8,128)(2,1)S(1)} collective-permute-done((bf16[128,128]{1,0:T(8,128)(2,1)S(1)}, bf16[128,128]{1,0:T(8,128)(2,1)S(1)}, u32[]{:S(2)}, u32[]{:S(2)}) %collective-permute-start.10) | collective-permute-done | bytes 32800 | tf_op jit(solution)/shard_map/ppermute | solution.py:220
  55.1 4.1 %collective-permute-start.16 = (bf16[2,128,128]{2,1,0:T(8,128)(2,1)S(1)}, bf16[2,128,128]{2,1,0:T(8,128)(2,1)S(1)}, u32[]{:S(2)}, u32[]{:S(2)}) collective-permute-start(bf16[2,128,128]{2,1,0:T(8,128)(2,1)S(1)} %pad_maximum_fusion.3), channel_id=1, source_target_pairs={{0,8},{1,9},{2,10},{3,11},{4,12},{5,13},{6,14},{7,15},{8,0},{9,1},... | collective-permute-start | bytes 196616 | tf_op jit(solution)/shard_map/ppermute | solution.py:220
  59.2 2.6 %collective-permute-start.17 = (bf16[2,128,128]{2,1,0:T(8,128)(2,1)S(1)}, bf16[2,128,128]{2,1,0:T(8,128)(2,1)S(1)}, u32[]{:S(2)}, u32[]{:S(2)}) collective-permute-start(bf16[2,128,128]{2,1,0:T(8,128)(2,1)S(1)} %slice.49), channel_id=1, source_target_pairs={{0,8},{1,9},{2,10},{3,11},{4,12},{5,13},{6,14},{7,15},{8,0},{9,1},... | collective-permute-start | bytes 196616 | tf_op jit(solution)/shard_map/ppermute | solution.py:220
  61.8 2.2 %collective-permute-start.18 = (bf16[2,128,128]{2,1,0:T(8,128)(2,1)S(1)}, bf16[2,128,128]{2,1,0:T(8,128)(2,1)S(1)}, u32[]{:S(2)}, u32[]{:S(2)}) collective-permute-start(bf16[2,128,128]{2,1,0:T(8,128)(2,1)S(1)} %slice.50), channel_id=1, source_target_pairs={{0,8},{1,9},{2,10},{3,11},{4,12},{5,13},{6,14},{7,15},{8,0},{9,1},... | collective-permute-start | bytes 196616 | tf_op jit(solution)/shard_map/ppermute | solution.py:220
  63.9 1.3 collective-permute-start.19
  66.2 2.8 %copy-done.4 = bf16[1024,3072]{1,0:T(8,128)(2,1)S(1)} copy-done((bf16[1024,3072]{1,0:T(8,128)(2,1)S(1)}, bf16[1024,3072]{1,0:T(8,128)(2,1)}, u32[]{:S(2)}) %copy-start.4) | copy-done | bytes 6291480
  68.9 4.0 %second_layer.1 = f32[16,128]{1,0:T(8,128)S(1)} custom-call(s32[8]{0:T(128)S(1)} %concatenate.11.scal_ref, bf16[4,128,128]{2,1,0:T(8,128)(2,1)S(1)} %pad_maximum_fusion.1.y0, bf16[4,128,128]{2,1,0:T(8,128)(2,1)S(1)} %collective-permute-done.13.y1, bf16[4,128,128]{2,1,0:T(8,128)(2,1)S(1)} %collective-permute-done.14.y2, ...), custom_call_target="tpu_custom_call" | custom-call | flops 1000000000 | bytes 1048576 | tf_op jit(solution)/shard_map/second_layer/pallas_call | solution.py:53
  73.5 6.3 %all-to-all-start = ((f32[8,16,128]{2,1,0:T(8,128)}), f32[8,16,128]{2,1,0:T(8,128)S(1)}, u32[]{:S(2)}, u32[]{:S(2)}) async-start(f32[8,16,128]{2,1,0:T(8,128)} %broadcast_in_dim.21), calls=%async_computation | async-start | bytes 131072 | tf_op jit(solution)/shard_map/all_to_all | solution.py:322
  79.9 5.8 %phases.1.wave_ref = bf16[2048,1024]{1,0:T(8,128)(2,1)S(1)} custom-call(bf16[4,144,128]{2,1,0:T(8,128)(2,1)S(1)} %pad_maximum_fusion.y0, bf16[4,144,128]{2,1,0:T(8,128)(2,1)S(1)} %collective-permute-done.3.y1, bf16[4,144,128]{2,1,0:T(8,128)(2,1)S(1)} %collective-permute-done.4.y2, bf16[4,144,128]{2,1,0:T(8,128)(2,1)S(1)} %collective-permute-done.5.y3, ...), custom_call_target="tpu_custom_call" | custom-call | flops 2000000000 | bytes 1048576 | tf_op jit(solution)/shard_map/phases/pallas_call | solution.py:53
  85.7 2.0 %copy-done.1 = bf16[2048,1024]{1,0:T(8,128)(2,1)} copy-done((bf16[2048,1024]{1,0:T(8,128)(2,1)}, bf16[2048,1024]{1,0:T(8,128)(2,1)S(1)}, u32[]{:S(2)}) %copy-start.1) | copy-done | bytes 4194328
  87.6 1.3 %all-to-all-done.charge_ref = f32[8,16,128]{2,1,0:T(8,128)S(1)} async-done(((f32[8,16,128]{2,1,0:T(8,128)}), f32[8,16,128]{2,1,0:T(8,128)S(1)}, u32[]{:S(2)}, u32[]{:S(2)}) %all-to-all-start) | async-done | bytes 65568 | tf_op jit(solution)/shard_map/all_to_all | solution.py:322
  89.0 2.2 %copy-done.2 = bf16[2048,1024]{1,0:T(8,128)(2,1)S(1)} copy-done((bf16[2048,1024]{1,0:T(8,128)(2,1)S(1)}, bf16[2048,1024]{1,0:T(8,128)(2,1)}, u32[]{:S(2)}) %copy-start.2) | copy-done | bytes 4194328
  91.2 2.1 %structure.1 = (f32[32,1024]{1,0:T(8,128)S(1)}, f32[16,1024]{1,0:T(8,128)S(1)}) custom-call(s32[8]{0:T(128)S(1)} %fusion.1.place_ref, bf16[2048,1024]{1,0:T(8,128)(2,1)S(1)} %copy-done.2, f32[8,16,128]{2,1,0:T(8,128)S(1)} %all-to-all-done.charge_ref), custom_call_target="tpu_custom_call" | custom-call | flops 100000000 | bytes 1048576 | tf_op jit(solution)/shard_map/structure/pallas_call | solution.py:53
  93.3 1.9 %collective-permute-start.20 = (f32[32,512]{1,0:T(8,128)S(1)}, f32[32,512]{1,0:T(8,128)S(1)}, u32[]{:S(2)}, u32[]{:S(2)}) collective-permute-start(f32[32,512]{1,0:T(8,128)S(1)} %slice_select_fusion), channel_id=1, source_target_pairs={{0,8},{1,9},{2,10},{3,11},{4,12},{5,13},{6,14},{7,15},{8,0},{9,1},... | collective-permute-start | bytes 196616 | tf_op jit(solution)/shard_map/ppermute | solution.py:220
  96.5 3.2 %collective-permute-start.23 = (f32[32,512]{1,0:T(8,128)S(1)}, f32[32,512]{1,0:T(8,128)S(1)}, u32[]{:S(2)}, u32[]{:S(2)}) collective-permute-start(f32[32,512]{1,0:T(8,128)S(1)} %select_add_fusion), channel_id=1, source_target_pairs={{0,48},{1,49},{2,50},{3,51},{4,52},{5,53},{6,54},{7,55},{8,56},{9,... | collective-permute-start | bytes 196616 | tf_op jit(solution)/shard_map/ppermute | solution.py:220
  100.6 1.9 %collective-permute-done.23 = f32[32,512]{1,0:T(8,128)S(1)} collective-permute-done((f32[32,512]{1,0:T(8,128)S(1)}, f32[32,512]{1,0:T(8,128)S(1)}, u32[]{:S(2)}, u32[]{:S(2)}) %collective-permute-start.23) | collective-permute-done | bytes 65568 | tf_op jit(solution)/shard_map/ppermute | solution.py:220
  103.3 1.8 %collective-permute-start.25 = (f32[32,512]{1,0:T(8,128)S(1)}, f32[32,512]{1,0:T(8,128)S(1)}, u32[]{:S(2)}, u32[]{:S(2)}) collective-permute-start(f32[32,512]{1,0:T(8,128)S(1)} %add_add_fusion.1), channel_id=1, source_target_pairs={{0,128},{1,129},{2,130},{3,131},{4,132},{5,133},{6,134},{7,135},{8... | collective-permute-start | bytes 196616 | tf_op jit(solution)/shard_map/ppermute | solution.py:220
  105.0 1.4 %collective-permute-start.26 = (f32[32,512]{1,0:T(8,128)S(1)}, f32[32,512]{1,0:T(8,128)S(1)}, u32[]{:S(2)}, u32[]{:S(2)}) collective-permute-start(f32[32,512]{1,0:T(8,128)S(1)} %add_add_fusion.1), channel_id=1, source_target_pairs={{0,192},{1,193},{2,194},{3,195},{4,196},{5,197},{6,198},{7,199},{8... | collective-permute-start | bytes 196616 | tf_op jit(solution)/shard_map/ppermute | solution.py:220
  108.2 4.4 %collective-permute-start.27 = (f32[32,512]{1,0:T(8,128)S(1)}, f32[32,512]{1,0:T(8,128)S(1)}, u32[]{:S(2)}, u32[]{:S(2)}) collective-permute-start(f32[32,512]{1,0:T(8,128)S(1)} %add_add_fusion), channel_id=1, source_target_pairs={{0,8},{1,9},{2,10},{3,11},{4,12},{5,13},{6,14},{7,15},{8,0},{9,1},... | collective-permute-start | bytes 196616 | tf_op jit(solution)/shard_map/ppermute | solution.py:220
  114.8 16.0 %all_to_all.10 = f32[8,24,128]{2,1,0:T(8,128)S(1)} all-to-all(f32[8,24,128]{2,1,0:T(8,128)S(1)} %respond.1), channel_id=1, replica_groups=mesh['slab'=32,'kgrp'=8] {'kgrp'}, dimensions={0} | all-to-all | bytes 196608 | tf_op jit(solution)/shard_map/all_to_all | solution.py:351
  (92 shorter events, 19.7 us)
Async XLA Ops:
  0.6 33.8 %copy-start.5 = (bf16[2,128,128]{2,1,0:T(8,128)(2,1)S(1)}, bf16[2,128,128]{2,1,0:T(8,128)(2,1)}, u32[]{:S(2)}) copy-start(bf16[2,128,128]{2,1,0:T(8,128)(2,1)} %node_ref.3) | copy-start | bytes 196612
  2.1 32.4 %copy-start.11 = (bf16[2,128,128]{2,1,0:T(8,128)(2,1)S(1)}, bf16[2,128,128]{2,1,0:T(8,128)(2,1)}, u32[]{:S(2)}) copy-start(bf16[2,128,128]{2,1,0:T(8,128)(2,1)} %edge_ref.1) | copy-start | bytes 196612
  2.1 10.1 %collective-permute-start = (bf16[144,128]{1,0:T(8,128)(2,1)S(1)}, bf16[144,128]{1,0:T(8,128)(2,1)S(1)}, u32[]{:S(2)}, u32[]{:S(2)}) collective-permute-start(bf16[144,128]{1,0:T(8,128)(2,1)S(1)} %pack.1), channel_id=1, source_target_pairs={{0,1},{1,0},{2,3},{3,2},{4,5},{5,4},{6,7},{7,6},{8,9},{9,8},{10,11... | collective-permute-start | bytes 110600 | tf_op jit(solution)/shard_map/ppermute | solution.py:220
  10.0 5.0 %collective-permute-start.1 = (bf16[144,128]{1,0:T(8,128)(2,1)S(1)}, bf16[144,128]{1,0:T(8,128)(2,1)S(1)}, u32[]{:S(2)}, u32[]{:S(2)}) collective-permute-start(bf16[144,128]{1,0:T(8,128)(2,1)S(1)} %pack.1), channel_id=1, source_target_pairs={{0,248},{1,249},{2,250},{3,251},{4,252},{5,253},{6,254},{7,255},{8... | collective-permute-start | bytes 110600 | tf_op jit(solution)/shard_map/ppermute | solution.py:220
  11.6 6.5 %collective-permute-start.2 = (bf16[144,128]{1,0:T(8,128)(2,1)S(1)}, bf16[144,128]{1,0:T(8,128)(2,1)S(1)}, u32[]{:S(2)}, u32[]{:S(2)}) collective-permute-start(bf16[144,128]{1,0:T(8,128)(2,1)S(1)} %pack.1), channel_id=1, source_target_pairs={{0,249},{1,248},{2,251},{3,250},{4,253},{5,252},{6,255},{7,254},{8... | collective-permute-start | bytes 110600 | tf_op jit(solution)/shard_map/ppermute | solution.py:220
  18.1 10.1 %collective-permute-start.3 = (bf16[4,144,128]{2,1,0:T(8,128)(2,1)S(1)}, bf16[4,144,128]{2,1,0:T(8,128)(2,1)S(1)}, u32[]{:S(2)}, u32[]{:S(2)}) collective-permute-start(bf16[4,144,128]{2,1,0:T(8,128)(2,1)S(1)} %pad_maximum_fusion.y0), channel_id=1, source_target_pairs={{0,6},{1,7},{2,0},{3,1},{4,2},{5,3},{6,4},{7,5},{8,14},{9,15},{10,... | collective-permute-start | bytes 442376 | tf_op jit(solution)/shard_map/ppermute | solution.py:220
  20.9 7.8 %collective-permute-start.4 = (bf16[4,144,128]{2,1,0:T(8,128)(2,1)S(1)}, bf16[4,144,128]{2,1,0:T(8,128)(2,1)S(1)}, u32[]{:S(2)}, u32[]{:S(2)}) collective-permute-start(bf16[4,144,128]{2,1,0:T(8,128)(2,1)S(1)} %pad_maximum_fusion.y0), channel_id=1, source_target_pairs={{0,4},{1,5},{2,6},{3,7},{4,0},{5,1},{6,2},{7,3},{8,12},{9,13},{10,... | collective-permute-start | bytes 442376 | tf_op jit(solution)/shard_map/ppermute | solution.py:220
  21.2 9.9 %collective-permute-start.5 = (bf16[4,144,128]{2,1,0:T(8,128)(2,1)S(1)}, bf16[4,144,128]{2,1,0:T(8,128)(2,1)S(1)}, u32[]{:S(2)}, u32[]{:S(2)}) collective-permute-start(bf16[4,144,128]{2,1,0:T(8,128)(2,1)S(1)} %pad_maximum_fusion.y0), channel_id=1, source_target_pairs={{0,2},{1,3},{2,4},{3,5},{4,6},{5,7},{6,0},{7,1},{8,10},{9,11},{10,... | collective-permute-start | bytes 442376 | tf_op jit(solution)/shard_map/ppermute | solution.py:220
  24.1 10.4 %collective-permute-start.6 = (bf16[2,144,128]{2,1,0:T(8,128)(2,1)S(1)}, bf16[2,144,128]{2,1,0:T(8,128)(2,1)S(1)}, u32[]{:S(2)}, u32[]{:S(2)}) collective-permute-start(bf16[2,144,128]{2,1,0:T(8,128)(2,1)S(1)} %pad_maximum_fusion.2), channel_id=1, source_target_pairs={{0,8},{1,9},{2,10},{3,11},{4,12},{5,13},{6,14},{7,15},{8,0},{9,1},... | collective-permute-start | bytes 221192 | tf_op jit(solution)/shard_map/ppermute | solution.py:220
  28.2 6.2 %collective-permute-start.7 = (bf16[2,144,128]{2,1,0:T(8,128)(2,1)S(1)}, bf16[2,144,128]{2,1,0:T(8,128)(2,1)S(1)}, u32[]{:S(2)}, u32[]{:S(2)}) collective-permute-start(bf16[2,144,128]{2,1,0:T(8,128)(2,1)S(1)} %slice.46), channel_id=1, source_target_pairs={{0,8},{1,9},{2,10},{3,11},{4,12},{5,13},{6,14},{7,15},{8,0},{9,1},... | collective-permute-start | bytes 221192 | tf_op jit(solution)/shard_map/ppermute | solution.py:220
  28.6 5.8 %collective-permute-start.8 = (bf16[2,144,128]{2,1,0:T(8,128)(2,1)S(1)}, bf16[2,144,128]{2,1,0:T(8,128)(2,1)S(1)}, u32[]{:S(2)}, u32[]{:S(2)}) collective-permute-start(bf16[2,144,128]{2,1,0:T(8,128)(2,1)S(1)} %slice.47), channel_id=1, source_target_pairs={{0,8},{1,9},{2,10},{3,11},{4,12},{5,13},{6,14},{7,15},{8,0},{9,1},... | collective-permute-start | bytes 221192 | tf_op jit(solution)/shard_map/ppermute | solution.py:220
  31.1 35.0 %copy-start.10 = (bf16[128,16]{0,1:T(8,128)(2,1)S(1)}, bf16[128,16]{0,1:T(8,128)(2,1)}, u32[]{:S(2)}) copy-start(bf16[128,16]{0,1:T(8,128)(2,1)} %param.19) | copy-start | bytes 12292
  31.1 3.3 %collective-permute-start.9 = (bf16[2,144,128]{2,1,0:T(8,128)(2,1)S(1)}, bf16[2,144,128]{2,1,0:T(8,128)(2,1)S(1)}, u32[]{:S(2)}, u32[]{:S(2)}) collective-permute-start(bf16[2,144,128]{2,1,0:T(8,128)(2,1)S(1)} %slice.48), channel_id=1, source_target_pairs={{0,8},{1,9},{2,10},{3,11},{4,12},{5,13},{6,14},{7,15},{8,0},{9,1},... | collective-permute-start | bytes 221192 | tf_op jit(solution)/shard_map/ppermute | solution.py:220
  44.9 7.5 %collective-permute-start.10 = (bf16[128,128]{1,0:T(8,128)(2,1)S(1)}, bf16[128,128]{1,0:T(8,128)(2,1)S(1)}, u32[]{:S(2)}, u32[]{:S(2)}) collective-permute-start(bf16[128,128]{1,0:T(8,128)(2,1)S(1)} %get-tuple-element.7), channel_id=1, source_target_pairs={{0,1},{1,0},{2,3},{3,2},{4,5},{5,4},{6,7},{7,6},{8,9},{9,8},{10,11... | collective-permute-start | bytes 98312 | tf_op jit(solution)/shard_map/ppermute | solution.py:220
  45.9 6.5 %collective-permute-start.11 = (bf16[128,128]{1,0:T(8,128)(2,1)S(1)}, bf16[128,128]{1,0:T(8,128)(2,1)S(1)}, u32[]{:S(2)}, u32[]{:S(2)}) collective-permute-start(bf16[128,128]{1,0:T(8,128)(2,1)S(1)} %get-tuple-element.7), channel_id=1, source_target_pairs={{0,248},{1,249},{2,250},{3,251},{4,252},{5,253},{6,254},{7,255},{8... | collective-permute-start | bytes 98312 | tf_op jit(solution)/shard_map/ppermute | solution.py:220
  46.4 6.8 %collective-permute-start.12 = (bf16[128,128]{1,0:T(8,128)(2,1)S(1)}, bf16[128,128]{1,0:T(8,128)(2,1)S(1)}, u32[]{:S(2)}, u32[]{:S(2)}) collective-permute-start(bf16[128,128]{1,0:T(8,128)(2,1)S(1)} %get-tuple-element.7), channel_id=1, source_target_pairs={{0,249},{1,248},{2,251},{3,250},{4,253},{5,252},{6,255},{7,254},{8... | collective-permute-start | bytes 98312 | tf_op jit(solution)/shard_map/ppermute | solution.py:220
  53.3 5.9 %collective-permute-start.13 = (bf16[4,128,128]{2,1,0:T(8,128)(2,1)S(1)}, bf16[4,128,128]{2,1,0:T(8,128)(2,1)S(1)}, u32[]{:S(2)}, u32[]{:S(2)}) collective-permute-start(bf16[4,128,128]{2,1,0:T(8,128)(2,1)S(1)} %pad_maximum_fusion.1.y0), channel_id=1, source_target_pairs={{0,6},{1,7},{2,0},{3,1},{4,2},{5,3},{6,4},{7,5},{8,14},{9,15},{10,... | collective-permute-start | bytes 393224 | tf_op jit(solution)/shard_map/ppermute | solution.py:220
  53.7 8.1 %collective-permute-start.14 = (bf16[4,128,128]{2,1,0:T(8,128)(2,1)S(1)}, bf16[4,128,128]{2,1,0:T(8,128)(2,1)S(1)}, u32[]{:S(2)}, u32[]{:S(2)}) collective-permute-start(bf16[4,128,128]{2,1,0:T(8,128)(2,1)S(1)} %pad_maximum_fusion.1.y0), channel_id=1, source_target_pairs={{0,4},{1,5},{2,6},{3,7},{4,0},{5,1},{6,2},{7,3},{8,12},{9,13},{10,... | collective-permute-start | bytes 393224 | tf_op jit(solution)/shard_map/ppermute | solution.py:220
  54.0 9.9 %collective-permute-start.15 = (bf16[4,128,128]{2,1,0:T(8,128)(2,1)S(1)}, bf16[4,128,128]{2,1,0:T(8,128)(2,1)S(1)}, u32[]{:S(2)}, u32[]{:S(2)}) collective-permute-start(bf16[4,128,128]{2,1,0:T(8,128)(2,1)S(1)} %pad_maximum_fusion.1.y0), channel_id=1, source_target_pairs={{0,2},{1,3},{2,4},{3,5},{4,6},{5,7},{6,0},{7,1},{8,10},{9,11},{10,... | collective-permute-start | bytes 393224 | tf_op jit(solution)/shard_map/ppermute | solution.py:220
  55.1 10.2 %collective-permute-start.16 = (bf16[2,128,128]{2,1,0:T(8,128)(2,1)S(1)}, bf16[2,128,128]{2,1,0:T(8,128)(2,1)S(1)}, u32[]{:S(2)}, u32[]{:S(2)}) collective-permute-start(bf16[2,128,128]{2,1,0:T(8,128)(2,1)S(1)} %pad_maximum_fusion.3), channel_id=1, source_target_pairs={{0,8},{1,9},{2,10},{3,11},{4,12},{5,13},{6,14},{7,15},{8,0},{9,1},... | collective-permute-start | bytes 196616 | tf_op jit(solution)/shard_map/ppermute | solution.py:220
  59.2 6.1 %collective-permute-start.17 = (bf16[2,128,128]{2,1,0:T(8,128)(2,1)S(1)}, bf16[2,128,128]{2,1,0:T(8,128)(2,1)S(1)}, u32[]{:S(2)}, u32[]{:S(2)}) collective-permute-start(bf16[2,128,128]{2,1,0:T(8,128)(2,1)S(1)} %slice.49), channel_id=1, source_target_pairs={{0,8},{1,9},{2,10},{3,11},{4,12},{5,13},{6,14},{7,15},{8,0},{9,1},... | collective-permute-start | bytes 196616 | tf_op jit(solution)/shard_map/ppermute | solution.py:220
  61.8 3.5 %collective-permute-start.18 = (bf16[2,128,128]{2,1,0:T(8,128)(2,1)S(1)}, bf16[2,128,128]{2,1,0:T(8,128)(2,1)S(1)}, u32[]{:S(2)}, u32[]{:S(2)}) collective-permute-start(bf16[2,128,128]{2,1,0:T(8,128)(2,1)S(1)} %slice.50), channel_id=1, source_target_pairs={{0,8},{1,9},{2,10},{3,11},{4,12},{5,13},{6,14},{7,15},{8,0},{9,1},... | collective-permute-start | bytes 196616 | tf_op jit(solution)/shard_map/ppermute | solution.py:220
  63.9 2.2 %collective-permute-start.19 = (bf16[2,128,128]{2,1,0:T(8,128)(2,1)S(1)}, bf16[2,128,128]{2,1,0:T(8,128)(2,1)S(1)}, u32[]{:S(2)}, u32[]{:S(2)}) collective-permute-start(bf16[2,128,128]{2,1,0:T(8,128)(2,1)S(1)} %slice.51), channel_id=1, source_target_pairs={{0,8},{1,9},{2,10},{3,11},{4,12},{5,13},{6,14},{7,15},{8,0},{9,1},... | collective-permute-start | bytes 196616 | tf_op jit(solution)/shard_map/ppermute | solution.py:220
  73.5 15.4 %all-to-all-start = ((f32[8,16,128]{2,1,0:T(8,128)}), f32[8,16,128]{2,1,0:T(8,128)S(1)}, u32[]{:S(2)}, u32[]{:S(2)}) async-start(f32[8,16,128]{2,1,0:T(8,128)} %broadcast_in_dim.21), calls=%async_computation | async-start | bytes 131072 | tf_op jit(solution)/shard_map/all_to_all | solution.py:322
  93.3 2.8 %collective-permute-start.20 = (f32[32,512]{1,0:T(8,128)S(1)}, f32[32,512]{1,0:T(8,128)S(1)}, u32[]{:S(2)}, u32[]{:S(2)}) collective-permute-start(f32[32,512]{1,0:T(8,128)S(1)} %slice_select_fusion), channel_id=1, source_target_pairs={{0,8},{1,9},{2,10},{3,11},{4,12},{5,13},{6,14},{7,15},{8,0},{9,1},... | collective-permute-start | bytes 196616 | tf_op jit(solution)/shard_map/ppermute | solution.py:220
  96.1 3.6 %collective-permute-start.21 = (f32[32,512]{1,0:T(8,128)S(1)}, f32[32,512]{1,0:T(8,128)S(1)}, u32[]{:S(2)}, u32[]{:S(2)}) collective-permute-start(f32[32,512]{1,0:T(8,128)S(1)} %select_add_fusion), channel_id=1, source_target_pairs={{0,16},{1,17},{2,18},{3,19},{4,20},{5,21},{6,22},{7,23},{8,24},{9,... | collective-permute-start | bytes 196616 | tf_op jit(solution)/shard_map/ppermute | solution.py:220
  96.2 4.4 %collective-permute-start.22 = (f32[32,512]{1,0:T(8,128)S(1)}, f32[32,512]{1,0:T(8,128)S(1)}, u32[]{:S(2)}, u32[]{:S(2)}) collective-permute-start(f32[32,512]{1,0:T(8,128)S(1)} %select_add_fusion), channel_id=1, source_target_pairs={{0,32},{1,33},{2,34},{3,35},{4,36},{5,37},{6,38},{7,39},{8,40},{9,... | collective-permute-start | bytes 196616 | tf_op jit(solution)/shard_map/ppermute | solution.py:220
  96.5 6.0 %collective-permute-start.23 = (f32[32,512]{1,0:T(8,128)S(1)}, f32[32,512]{1,0:T(8,128)S(1)}, u32[]{:S(2)}, u32[]{:S(2)}) collective-permute-start(f32[32,512]{1,0:T(8,128)S(1)} %select_add_fusion), channel_id=1, source_target_pairs={{0,48},{1,49},{2,50},{3,51},{4,52},{5,53},{6,54},{7,55},{8,56},{9,... | collective-permute-start | bytes 196616 | tf_op jit(solution)/shard_map/ppermute | solution.py:220
  102.5 4.4 %collective-permute-start.24 = (f32[32,512]{1,0:T(8,128)S(1)}, f32[32,512]{1,0:T(8,128)S(1)}, u32[]{:S(2)}, u32[]{:S(2)}) collective-permute-start(f32[32,512]{1,0:T(8,128)S(1)} %add_add_fusion.1), channel_id=1, source_target_pairs={{0,64},{1,65},{2,66},{3,67},{4,68},{5,69},{6,70},{7,71},{8,72},{9,... | collective-permute-start | bytes 196616 | tf_op jit(solution)/shard_map/ppermute | solution.py:220
  103.3 4.6 %collective-permute-start.25 = (f32[32,512]{1,0:T(8,128)S(1)}, f32[32,512]{1,0:T(8,128)S(1)}, u32[]{:S(2)}, u32[]{:S(2)}) collective-permute-start(f32[32,512]{1,0:T(8,128)S(1)} %add_add_fusion.1), channel_id=1, source_target_pairs={{0,128},{1,129},{2,130},{3,131},{4,132},{5,133},{6,134},{7,135},{8... | collective-permute-start | bytes 196616 | tf_op jit(solution)/shard_map/ppermute | solution.py:220
  105.0 3.2 %collective-permute-start.26 = (f32[32,512]{1,0:T(8,128)S(1)}, f32[32,512]{1,0:T(8,128)S(1)}, u32[]{:S(2)}, u32[]{:S(2)}) collective-permute-start(f32[32,512]{1,0:T(8,128)S(1)} %add_add_fusion.1), channel_id=1, source_target_pairs={{0,192},{1,193},{2,194},{3,195},{4,196},{5,197},{6,198},{7,199},{8... | collective-permute-start | bytes 196616 | tf_op jit(solution)/shard_map/ppermute | solution.py:220
  108.2 5.3 %collective-permute-start.27 = (f32[32,512]{1,0:T(8,128)S(1)}, f32[32,512]{1,0:T(8,128)S(1)}, u32[]{:S(2)}, u32[]{:S(2)}) collective-permute-start(f32[32,512]{1,0:T(8,128)S(1)} %add_add_fusion), channel_id=1, source_target_pairs={{0,8},{1,9},{2,10},{3,11},{4,12},{5,13},{6,14},{7,15},{8,0},{9,1},... | collective-permute-start | bytes 196616 | tf_op jit(solution)/shard_map/ppermute | solution.py:220
  (9 other events, 85.3 us)

commit v2 on v1

v2 whole, which is shorter than its diff:
```python
import math

import jax
import jax.numpy as jnp
from jax import lax
from jax.experimental import pallas as pl
from jax.experimental.pallas import tpu as pltpu
from jax.sharding import PartitionSpec as P

AXES = ("slab", "kgrp")
F32 = jnp.float32
BF16 = jnp.bfloat16
MIB = 1 << 20

ROWS = 128
PAYLOAD = 144

CENTRE = 3.04
SINC = (4.53143365e-01, -1.10011030e-01, 6.70800349e-03, -1.85302418e-04, 2.92602795e-06, -2.98676509e-08)
TWOCOS = (-5.04597246e-01, -5.81178942e-01, 7.05473141e-02, -2.86778430e-03, 5.94149034e-05, -7.50432042e-07, 6.38391477e-09)
SINTURN = (6.2831853, -41.34170041, 81.60513139, -76.70301535, 42.02592698, -14.89984666, 3.2381375)
COSTURN = (0.99999999, -19.7392045, 64.93911746, -85.45013953, 60.16763095, -25.96759925, 6.52865816)


def horner(coefficients, x):
    value = coefficients[-1] * x + coefficients[-2]
    for c in coefficients[-3::-1]:
        value = value * x + c
    return value


def split(x, parts):
    pieces = []
    for i in range(parts):
        piece = x.astype(BF16)
        pieces.append(piece)
        if i + 1 < parts:
            x = x - piece.astype(F32)
    return pieces


def nt(a, b):
    return lax.dot_general(a, b, (((1,), (1,)), ((), ())), preferred_element_type=F32)


def nn(a, b):
    return jnp.dot(a, b, preferred_element_type=F32)


def call(body, out_shape, *operands, scalars=(), after=(), name, flops=0, limit=12, scratch=()):
    n, m = len(scalars) + len(operands), len(after)
    return pl.pallas_call(
        lambda *refs: body(*refs[:n], *refs[n + m :]),
        out_shape=out_shape,
        in_specs=[pl.BlockSpec(memory_space=pltpu.SMEM)] * len(scalars)
        + [pl.BlockSpec(memory_space=pltpu.VMEM)] * len(operands)
        + [pl.BlockSpec(memory_space=pl.ANY)] * m,
        scratch_shapes=list(scratch),
        name=name,
        cost_estimate=pl.CostEstimate(flops=flops, bytes_accessed=MIB, transcendentals=0),
        compiler_params=pltpu.CompilerParams(vmem_limit_bytes=limit * MIB),
    )(*scalars, *operands, *after)


def pack_body(desc_ref, loc_ref, out_ref):
    out_ref[0:ROWS, :] = desc_ref[...]
    hi, mid, lo = [p.astype(F32) for p in split(loc_ref[...], 3)]
    tail = jnp.concatenate([hi, mid, lo, jnp.zeros((7, ROWS), F32)], axis=0)
    out_ref[ROWS:PAYLOAD, :] = tail.astype(BF16)


def coordinates(payload):
    tail = payload[ROWS:PAYLOAD, :].astype(F32)
    return (tail[0:3] + tail[3:6]) + tail[6:9]


def count_body(scal_ref, slots_ref, tally_ref, *cnt_refs):
    y, zh, odd = scal_ref[0], scal_ref[1], scal_ref[2]
    f_prev, f_own, f_next, base = scal_ref[3], scal_ref[4], scal_ref[5], scal_ref[6]
    slots = slots_ref[...]
    shape = slots.shape
    lane = lax.broadcasted_iota(jnp.int32, shape, 1)
    row = lax.broadcasted_iota(jnp.int32, shape, 0)
    local = lane >> 6
    atom = row * 8 + local + base
    region = slots >> 10
    within = slots & 1023
    filled = jnp.where(region == 0, f_prev, jnp.where(region == 1, f_own, f_next))
    usable = ((lane & 63) < tally_ref[...]) & (within < filled) & (atom < f_own)
    kblock = within >> 7
    place = jnp.where(region == 1, 0, jnp.where(region == 2 * odd, 2, 4)) + ((kblock & 1) ^ zh)
    target = jnp.where(usable, ((((kblock >> 1) - y) & 3) * 6 + place) * 8 + local, -1)
    low = slots & 127
    iota_p = lax.broadcasted_iota(jnp.int32, (192, 512), 0)
    iota_l = lax.broadcasted_iota(jnp.int32, (128, 512), 0)
    for i in range(16):
        p = jnp.where(iota_p == target[i : i + 1], 1.0, 0.0).astype(BF16)
        l = jnp.where(iota_l == low[i : i + 1], 1.0, 0.0).astype(BF16)
        c = nt(p, l).reshape(24, 8, 128)
        for j in range(4):
            cnt_refs[j][:, 8 * i : 8 * i + 8, :] = c[6 * j : 6 * j + 6]


def update(gathered, hidden, self_weight):
    drive = gathered * 0.125 + nn(hidden, self_weight)
    return (hidden.astype(F32) + drive * jax.nn.sigmoid(drive)).astype(BF16)


def mix(acc, mixing):
    total = acc[0:ROWS] * mixing[0:1]
    for n in range(1, 8):
        total = total + acc[n * ROWS : (n + 1) * ROWS] * mixing[n : n + 1]
    return total


def block_of(y_ref, c_ref, i):
    return y_ref[i] if i < 4 else c_ref[i - 4]


def basis_part(shift_ref, y_ref, c_ref, cnt_ref, here_ref, edge_ref, mixing_ref, g_ref):
    rows = []
    for i in range(6):
        payload = block_of(y_ref, c_ref, i)
        rows.append(nn(payload[0:ROWS, :], edge_ref[0]).astype(BF16))
        xyz = coordinates(payload)
        x = xyz[0:1] + shift_ref[i // 2]
        for r in range(0, ROWS, 64):
            here = here_ref[r : r + 64, :]
            dx = x - here[:, 0:1]
            dy = xyz[1:2] - here[:, 1:2]
            dz = xyz[2:3] - here[:, 2:3]
            v = dx * dx + dy * dy + dz * dz + (0.04 - CENTRE)
            cur = cnt_ref[i, r : r + 64, :] * horner(SINC, v)
            turn = horner(TWOCOS, v)
            prev = None
            for n in range(8):
                g_ref[n * ROWS + r : n * ROWS + r + 64, i * 128 : (i + 1) * 128] = cur.astype(BF16)
                nxt = turn * cur if prev is None else turn * cur - prev
                prev, cur = cur, nxt
    return mix(nn(g_ref[...], jnp.concatenate(rows, axis=0)), mixing_ref[0])


def first_body(shift_ref, y_ref, c_ref, cnt_ref, here_ref, edge_ref, mixing_ref, g_ref, part_ref):
    part_ref[...] = basis_part(shift_ref, y_ref, c_ref, cnt_ref, here_ref, edge_ref, mixing_ref, g_ref)


def first_last_body(shift_ref, y_ref, c_ref, cnt_ref, here_ref, edge_ref, mixing_ref, p0, p1, p2, own_ref, node_ref, g_ref, hidden_ref, message_ref):
    gathered = basis_part(shift_ref, y_ref, c_ref, cnt_ref, here_ref, edge_ref, mixing_ref, g_ref)
    gathered = ((p0[...] + p1[...]) + p2[...]) + gathered
    hidden = update(gathered, own_ref[0, 0:ROWS, :], node_ref[0])
    hidden_ref[...] = hidden
    message_ref[...] = nn(hidden, edge_ref[1]).astype(BF16)


def gather_part(y_ref, c_ref, g_ref):
    return nn(g_ref[...], jnp.concatenate([block_of(y_ref, c_ref, i) for i in range(6)], axis=0))


def second_body(y_ref, c_ref, g_ref, mixing_ref, part_ref):
    part_ref[...] = mix(gather_part(y_ref, c_ref, g_ref), mixing_ref[1])


def second_last_body(scal_ref, y_ref, c_ref, g_ref, mixing_ref, p0, p1, p2, hidden_ref, node_ref, readout_ref, charge_ref):
    gathered = ((p0[...] + p1[...]) + p2[...]) + mix(gather_part(y_ref, c_ref, g_ref), mixing_ref[1])
    hidden = update(gathered, hidden_ref[...], node_ref[1])
    charges = nt(readout_ref[...], hidden)
    atom = lax.broadcasted_iota(jnp.int32, charges.shape, 1) + scal_ref[6]
    charges = jnp.where(atom < scal_ref[4], charges, 0.0)
    for i in range(8):
        charge_ref[i] = charges


def stack_body(a, b, c, d, out_ref):
    for i, ref in enumerate((a, b, c, d)):
        out_ref[i] = ref[...]


def phase_body(y_ref, modes_ref, wave_ref):
    for b in range(2):
        xyz = coordinates(y_ref[b])
        for r in range(0, 1024, 64):
            k = modes_ref[r : r + 64, :]
            turns = k[:, 0:1] * xyz[0:1] + k[:, 1:2] * xyz[1:2] + k[:, 2:3] * xyz[2:3]
            rest = turns - jnp.round(turns)
            square = rest * rest
            wave_ref[r : r + 64, b * 128 : (b + 1) * 128] = horner(COSTURN, square).astype(BF16)
            wave_ref[1024 + r : 1024 + r + 64, b * 128 : (b + 1) * 128] = (rest * horner(SINTURN, square)).astype(BF16)


def structure_body(place_ref, w0, w1, w2, w3, charge_ref, out_ref, q_ref):
    charges = jnp.concatenate([charge_ref[place_ref[b]] for b in range(8)], axis=1)
    q_ref[...] = charges
    pieces = jnp.concatenate(split(charges, 3), axis=0)
    for i in range(2):
        for r in range(i * 1024, (i + 1) * 1024, 256):
            s = nt(w0[r : r + 256, :], pieces[:, 0:256])
            for j, w in enumerate((w1, w2, w3), 1):
                s = s + nt(w[r : r + 256, :], pieces[:, j * 256 : (j + 1) * 256])
            s = s[:, 0:16] + s[:, 16:32] + s[:, 32:48]
            out_ref[i * 16 : (i + 1) * 16, r - i * 1024 : r - i * 1024 + 256] = s.T


def respond_body(place_ref, scale_ref, w0, w1, w2, w3, sum_ref, q_ref, modes_ref, out_ref):
    k = modes_ref[...]
    square = k[0:1] * k[0:1] + k[1:2] * k[1:2] + k[2:3] * k[2:3]
    weight = scale_ref[0] * jnp.exp(square * -0.125) / (square + 1.0)
    real = sum_ref[0:16, :] * weight
    imag = sum_ref[16:32, :] * weight
    left = [real] + [imag * k[j : j + 1] for j in range(3)]
    right = [imag] + [real * -k[j : j + 1] for j in range(3)]
    both = jnp.concatenate([jnp.concatenate(left, axis=0), jnp.concatenate(right, axis=0)], axis=1)
    pieces = jnp.concatenate(split(both, 2), axis=0)
    for i, w in enumerate((w0, w1, w2, w3)):
        out = nn(pieces, w[...])
        out = out[0:64] + out[64:128]
        q = q_ref[:, i * 256 : (i + 1) * 256]
        force = [-jnp.sum(out[16 * j + 16 : 16 * j + 32] * q, axis=0, keepdims=True) for j in range(3)]
        full = jnp.concatenate([out[0:16]] + force + [jnp.zeros((5, 256), F32)], axis=0)
        for b in range(2):
            out_ref[place_ref[2 * i + b]] = full[:, b * 128 : (b + 1) * 128]


def finish_body(parts_ref, potential_ref, forces_ref):
    total = parts_ref[0]
    for i in range(1, 8):
        total = total + parts_ref[i]
    potential_ref[...] = total[0:16]
    forces_ref[...] = total[16:19]


def pairs(n_slab, target):
    return [(s * 8 + k, (target(s, k)[0] % n_slab) * 8 + target(s, k)[1]) for s in range(n_slab) for k in range(8)]


def move(x, target):
    return lax.ppermute(x, AXES, pairs(lax.axis_size("slab"), target))


def over_chip(s):
    return s + 1 if s % 2 else s - 1


def near_blocks(block):
    half = move(block, lambda s, k: (s, k ^ 1))
    near = move(block, lambda s, k: (over_chip(s), k))
    both = move(block, lambda s, k: (over_chip(s), k ^ 1))
    return half, near, both


def surroundings(block, near, name, after):
    stack = call(stack_body, jax.ShapeDtypeStruct((4,) + block.shape, BF16), block, *near, name=name, after=after)
    ys = [stack]
    for j in range(1, 4):
        ys.append(move(stack, lambda s, k: (s, (k - 2 * j) % 8)))
    return ys, [move(y[0:2], lambda s, k: (s ^ 1, k)) for y in ys]


def shards(
    atom_descriptors,
    atom_locations,
    adjacent_atom_slots,
    neighbour_tally,
    filled_slot_tallies,
    reciprocal_lattice_modes,
    edge_update_matrix,
    node_update_matrix,
    distance_basis_mixing,
    latent_ionic_readout,
):
    n_slab = lax.axis_size("slab")
    slab = lax.axis_index("slab")
    group = lax.axis_index("kgrp")
    odd = slab % 2
    y, zh = group // 2, group % 2
    filled = jnp.take(filled_slot_tallies, (slab + jnp.arange(3) - 1) % n_slab)
    scal = jnp.concatenate([jnp.stack([y, zh, odd]), filled, jnp.stack([group * ROWS, 0])]).astype(jnp.int32)
    low_edge = jnp.where(slab == 0, -float(n_slab), 0.0)
    high_edge = jnp.where(slab == n_slab - 1, float(n_slab), 0.0)
    shift = jnp.stack([0.0, jnp.where(odd == 1, high_edge, low_edge), jnp.where(odd == 1, low_edge, high_edge)]).astype(F32)
    spots = jnp.arange(8, dtype=jnp.int32)
    place = (((y + spots // 2) % 4) * 2 + ((spots % 2) ^ zh)).astype(jnp.int32)

    shape = jax.ShapeDtypeStruct
    block = call(pack_body, shape((PAYLOAD, ROWS), BF16), atom_descriptors, atom_locations, name="pack")
    near = near_blocks(block)
    counts = call(
        count_body,
        [shape((6, ROWS, 128), F32)] * 4,
        adjacent_atom_slots.reshape(16, 512),
        jnp.broadcast_to(neighbour_tally[:, None], (ROWS, 64)).reshape(16, 512),
        scalars=(scal,),
        name="counts",
        flops=10**9,
    )
    ys, cs = surroundings(block, near, "stack_first", (counts[0],))
    here = atom_locations.T
    basis, parts = [None] * 4, [None] * 3
    for j in range(3):
        basis[j], parts[j] = call(
            first_body,
            (shape((8 * ROWS, 6 * ROWS), BF16), shape((ROWS, 128), F32)),
            ys[j], cs[j], counts[j], here, edge_update_matrix, distance_basis_mixing,
            scalars=(shift,),
            name=f"first_{j}",
            flops=10**9,
        )
    basis[3], hidden, messages = call(
        first_last_body,
        (shape((8 * ROWS, 6 * ROWS), BF16), shape((ROWS, 128), BF16), shape((ROWS, 128), BF16)),
        ys[3], cs[3], counts[3], here, edge_update_matrix, distance_basis_mixing, *parts, ys[0], node_update_matrix,
        scalars=(shift,),
        name="first_3",
        flops=10**9,
    )
    turns = reciprocal_lattice_modes.T * (0.5 / math.pi)

    def phases(j, after):
        return call(phase_body, shape((2048, 256), BF16), ys[j], turns, name=f"phases_{j}", flops=10**9, after=after)

    near = near_blocks(messages)
    waves = [phases(0, (messages,)), phases(1, (messages,))]
    ms, ns = surroundings(messages, near, "stack_second", waves)
    waves += [phases(2, (ms[0],)), phases(3, (ms[0],))]
    parts = [
        call(
            second_body,
            shape((ROWS, 128), F32),
            ms[j], ns[j], basis[j], distance_basis_mixing,
            name=f"second_{j}",
            flops=10**9,
            after=waves[2:] if j == 0 else (),
        )
        for j in range(3)
    ]
    charges = call(
        second_last_body,
        shape((8, 16, ROWS), F32),
        ms[3], ns[3], basis[3], distance_basis_mixing, *parts, hidden, node_update_matrix, latent_ionic_readout.T,
        scalars=(scal,),
        name="second_3",
        flops=10**9,
    )
    slab_charges = lax.all_to_all(charges, "kgrp", 0, 0)
    sums, q = call(
        structure_body,
        (shape((32, 1024), F32), shape((16, 1024), F32)),
        *waves,
        slab_charges,
        scalars=(place,),
        name="structure",
        flops=10**8,
    )
    lower, upper = sums[:, :512], sums[:, 512:]
    is_odd = odd == 1
    part = jnp.where(is_odd, upper, lower) + move(jnp.where(is_odd, lower, upper), lambda s, k: (s ^ 1, k))
    part = part + sum(move(part, lambda s, k, m=m: (s ^ (2 * m), k)) for m in (1, 2, 3))
    part = part + sum(move(part, lambda s, k, m=m: (s + 8 * m, k)) for m in (1, 2, 3))
    other = move(part, lambda s, k: (s ^ 1, k))
    total = jnp.where(is_odd, jnp.concatenate([other, part], axis=1), jnp.concatenate([part, other], axis=1))
    scale = jnp.full((1,), 4.0 / math.sqrt(n_slab * 1024 * reciprocal_lattice_modes.shape[1] * 8), F32)
    partial = call(
        respond_body,
        shape((8, 24, ROWS), F32),
        *waves,
        total,
        q,
        reciprocal_lattice_modes,
        scalars=(place, scale),
        name="respond",
        flops=10**8,
    )
    partial = lax.all_to_all(partial, "kgrp", 0, 0)
    return tuple(call(finish_body, (shape((16, ROWS), F32), shape((3, ROWS), F32)), partial, name="finish"))


def solution(mesh):
    return jax.shard_map(
        shards,
        mesh=mesh,
        in_specs=(
            P(("slab", "kgrp"), None),
            P(None, ("slab", "kgrp")),
            P(("slab", "kgrp"), None),
            P(("slab", "kgrp")),
            P(),
            P(None, "kgrp"),
            P(),
            P(),
            P(),
            P(),
        ),
        out_specs=(P(None, ("slab", "kgrp")), P(None, ("slab", "kgrp"))),
        check_vma=False,
    )
```

time: 133 us -> 115 us (0.86)
  local copies, waits for them, and re-layouts: 15.8 us -> 6 us
  starting transfers between devices: 59.5 us -> 54.3 us
  blocking collectives: 16 us -> 11.7 us
  waiting for transfers between devices: 16.8 us -> 18.3 us
    unnamed x26 -> x28, local copies, waits for them, and re-layouts: 12 us -> 4.04 us
    all_to_all x1, waiting for transfers between devices: 1.33 us -> 9.09 us  [shards(): slab_charges = lax.all_to_all(charges, 'kgrp', 0, 0)]
    ppermute x28, waiting for transfers between devices: 15.4 us -> 9.17 us  [move(): return lax.ppermute(x, AXES, pairs(lax.axis_size('slab'), target))]
    all_to_all x1, blocking collectives: 16 us -> 11.7 us  [shards(): partial = lax.all_to_all(partial, 'kgrp', 0, 0)]
    ppermute x28, starting transfers between devices: 53.2 us -> 49.7 us  [move(): return lax.ppermute(x, AXES, pairs(lax.axis_size('slab'), target))]
    all_to_all x1, starting transfers between devices: 6.33 us -> 4.61 us  [shards(): slab_charges = lax.all_to_all(charges, 'kgrp', 0, 0)]
    pallas_call x7 -> x19, Pallas kernels: 22.6 us -> 23.3 us  [call(): pl.pallas_call(lambda *refs: body(*refs[:n], *refs[n + m:]), out_shape=ou...]
  transfers between devices with their start and end apart: 29 -> 29, of which waited for: 13 -> 9; matrix products, arithmetic and copies ran while one was open for 2% -> 3% of each run, Pallas kernels for 6% -> 13%
where the time goes in v2:
time: 115 us
  starting transfers between devices  54.3 us (47%)
  Pallas kernels  23.3 us (20%)
  waiting for transfers between devices  18.3 us (16%)
  blocking collectives  11.7 us (10%)
  local copies, waits for them, and re-layouts  6 us (5%)
    ppermute x28, starting transfers between devices, move(): return lax.ppermute(x, AXES, pairs(lax.axis_size('slab'), target))  49.7 us
    pallas_call x19, Pallas kernels, call(): pl.pallas_call(lambda *refs: body(*refs[:n], *refs[n + m:]), out_shape=ou...  23.3 us
    all_to_all x1, blocking collectives, shards(): partial = lax.all_to_all(partial, 'kgrp', 0, 0)  11.7 us
    ppermute x28, waiting for transfers between devices, move(): return lax.ppermute(x, AXES, pairs(lax.axis_size('slab'), target))  9.17 us
    all_to_all x1, waiting for transfers between devices, shards(): slab_charges = lax.all_to_all(charges, 'kgrp', 0, 0)  9.09 us
    all_to_all x1, starting transfers between devices, shards(): slab_charges = lax.all_to_all(charges, 'kgrp', 0, 0)  4.61 us
    unnamed x28, local copies, waits for them, and re-layouts  4.04 us
  transfers between devices with their start and end apart: 29, of which 9 were waited for; matrix products, arithmetic and copies ran while one was open for 3% of the time, Pallas kernels for 13%

profile of v2, /device:TPU:1, one launch (start us, length us, event | category | flops | bytes accessed | tf_op | source)
XLA Modules:
  0.0 114.9 jit_solution(3770509933580198927)
XLA Ops:
  2.1 7.8 %collective-permute-start = (bf16[144,128]{1,0:T(8,128)(2,1)S(1)}, bf16[144,128]{1,0:T(8,128)(2,1)S(1)}, u32[]{:S(2)}, u32[]{:S(2)}) collective-permute-start(bf16[144,128]{1,0:T(8,128)(2,1)S(1)} %pack.1.refs_0_), channel_id=1, source_target_pairs={{0,1},{1,0},{2,3},{3,2},{4,5},{5,4},{6,7},{7,6},{8,9},{9,8},{10,11... | collective-permute-start | bytes 110600 | tf_op jit(solution)/shard_map/ppermute | solution.py:236
  9.9 1.6 %collective-permute-start.1 = (bf16[144,128]{1,0:T(8,128)(2,1)S(1)}, bf16[144,128]{1,0:T(8,128)(2,1)S(1)}, u32[]{:S(2)}, u32[]{:S(2)}) collective-permute-start(bf16[144,128]{1,0:T(8,128)(2,1)S(1)} %pack.1.refs_0_), channel_id=1, source_target_pairs={{0,248},{1,249},{2,250},{3,251},{4,252},{5,253},{6,254},{7,255},{8... | collective-permute-start | bytes 110600 | tf_op jit(solution)/shard_map/ppermute | solution.py:236
  14.1 1.6 %counts.1 = (f32[6,128,128]{2,1,0:T(8,128)S(1)}, f32[6,128,128]{2,1,0:T(8,128)S(1)}, f32[6,128,128]{2,1,0:T(8,128)S(1)}, f32[6,128,128]{2,1,0:T(8,128)S(1)}) custom-call(s32[8]{0:T(128)S(1)} %concatenate.9.refs_0_, s32[16,512]{1,0:T(8,128)S(1)} %reshape.69.refs_1_, s32[16,512]{1,0:T(8,128)S(1)} %broadcast_in_dim.14.refs_2_), custom_call_target="tpu_custom_call" | custom-call | flops 1000000000 | bytes 1048576 | tf_op jit(solution)/shard_map/counts/pallas_call | solution.py:52
  15.8 2.2 %collective-permute-done.2.refs_3_ = bf16[144,128]{1,0:T(8,128)(2,1)S(1)} collective-permute-done((bf16[144,128]{1,0:T(8,128)(2,1)S(1)}, bf16[144,128]{1,0:T(8,128)(2,1)S(1)}, u32[]{:S(2)}, u32[]{:S(2)}) %collective-permute-start.2) | collective-permute-done | bytes 36896 | tf_op jit(solution)/shard_map/ppermute | solution.py:236
  18.0 3.0 %collective-permute-start.8 = (bf16[4,144,128]{2,1,0:T(8,128)(2,1)S(1)}, bf16[4,144,128]{2,1,0:T(8,128)(2,1)S(1)}, u32[]{:S(2)}, u32[]{:S(2)}) collective-permute-start(bf16[4,144,128]{2,1,0:T(8,128)(2,1)S(1)} %stack_first.1.refs_1_.refs_10_.refs_0_), channel_id=1, source_target_pairs={{0,4},{1,5},{2,6},{3,7},{4,0},{5,1},{6,2},{7,3},{8,12},{9,13},{10,... | collective-permute-start | bytes 442376 | tf_op jit(solution)/shard_map/ppermute | solution.py:236
  22.6 4.0 %collective-permute-start.5 = (bf16[2,144,128]{2,1,0:T(8,128)(2,1)S(1)}, bf16[2,144,128]{2,1,0:T(8,128)(2,1)S(1)}, u32[]{:S(2)}, u32[]{:S(2)}) collective-permute-start(bf16[2,144,128]{2,1,0:T(8,128)(2,1)S(1)} %slice.43), channel_id=1, source_target_pairs={{0,8},{1,9},{2,10},{3,11},{4,12},{5,13},{6,14},{7,15},{8,0},{9,1},... | collective-permute-start | bytes 221192 | tf_op jit(solution)/shard_map/ppermute | solution.py:236
  28.2 2.0 %first_0.1 = (bf16[1024,768]{1,0:T(8,128)(2,1)S(1)}, f32[128,128]{1,0:T(8,128)S(1)}) custom-call(f32[3]{0:T(128)S(1)} %pad_maximum_fusion.refs_0_, bf16[4,144,128]{2,1,0:T(8,128)(2,1)S(1)} %stack_first.1.refs_1_.refs_10_.refs_0_, bf16[2,144,128]{2,1,0:T(8,128)(2,1)S(1)} %collective-permute-done.5.refs_2_, ...), custom_call_target="tpu_custom_call" | custom-call | flops 1000000000 | bytes 1048576 | tf_op jit(solution)/shard_map/first_0/pallas_call | solution.py:52
  30.4 1.6 %collective-permute-start.4 = (bf16[2,144,128]{2,1,0:T(8,128)(2,1)S(1)}, bf16[2,144,128]{2,1,0:T(8,128)(2,1)S(1)}, u32[]{:S(2)}, u32[]{:S(2)}) collective-permute-start(bf16[2,144,128]{2,1,0:T(8,128)(2,1)S(1)} %slice.42), channel_id=1, source_target_pairs={{0,8},{1,9},{2,10},{3,11},{4,12},{5,13},{6,14},{7,15},{8,0},{9,1},... | collective-permute-start | bytes 221192 | tf_op jit(solution)/shard_map/ppermute | solution.py:236
  32.0 2.0 %first_2.1 = (bf16[1024,768]{1,0:T(8,128)(2,1)S(1)}, f32[128,128]{1,0:T(8,128)S(1)}) custom-call(f32[3]{0:T(128)S(1)} %pad_maximum_fusion.refs_0_, bf16[4,144,128]{2,1,0:T(8,128)(2,1)S(1)} %collective-permute-done.8.refs_1_.refs_0_, bf16[2,144,128]{2,1,0:T(8,128)(2,1)S(1)} %collective-permute-done.9.refs_2_, f32[6,128,128]{2,1,0:T(8,128)S(1)} %get-tuple-element.22.refs_3_, ...), custom_call_target="tpu_custom_call" | custom-call | flops 1000000000 | bytes 1048576 | tf_op jit(solution)/shard_map/first_2/pallas_call | solution.py:52
  34.1 2.0 %first_1.1 = (bf16[1024,768]{1,0:T(8,128)(2,1)S(1)}, f32[128,128]{1,0:T(8,128)S(1)}) custom-call(f32[3]{0:T(128)S(1)} %pad_maximum_fusion.refs_0_, bf16[4,144,128]{2,1,0:T(8,128)(2,1)S(1)} %collective-permute-done.6.refs_1_.refs_0_, bf16[2,144,128]{2,1,0:T(8,128)(2,1)S(1)} %collective-permute-done.7.refs_2_, f32[6,128,128]{2,1,0:T(8,128)S(1)} %get-tuple-element.20.refs_3_, ...), custom_call_target="tpu_custom_call" | custom-call | flops 1000000000 | bytes 1048576 | tf_op jit(solution)/shard_map/first_1/pallas_call | solution.py:52
  36.1 2.2 %first_3.1 = (bf16[1024,768]{1,0:T(8,128)(2,1)S(1)}, bf16[128,128]{1,0:T(8,128)(2,1)S(1)}, bf16[128,128]{1,0:T(8,128)(2,1)S(1)}) custom-call(f32[3]{0:T(128)S(1)} %pad_maximum_fusion.refs_0_, bf16[4,144,128]{2,1,0:T(8,128)(2,1)S(1)} %collective-permute-done.3.refs_1_.refs_0_, bf16[2,144,128]{2,1,0:T(8,128)(2,1)S(1)} %collective-permute-done.4.refs_2_, ...), custom_call_target="tpu_custom_call" | custom-call | flops 1000000000 | bytes 1048576 | tf_op jit(solution)/shard_map/first_3/pallas_call | solution.py:52
  38.3 2.2 %collective-permute-start.10 = (bf16[128,128]{1,0:T(8,128)(2,1)S(1)}, bf16[128,128]{1,0:T(8,128)(2,1)S(1)}, u32[]{:S(2)}, u32[]{:S(2)}) collective-permute-start(bf16[128,128]{1,0:T(8,128)(2,1)S(1)} %get-tuple-element.24.refs_2_.refs_0_), channel_id=1, source_target_pairs={{0,1},{1,0},{2,3},{3,2},{4,5},{5,4},{6,7},{7,6},{8,9},{9,8},{10,11... | collective-permute-start | bytes 98312 | tf_op jit(solution)/shard_map/ppermute | solution.py:236
  40.4 3.9 %collective-permute-start.12 = (bf16[128,128]{1,0:T(8,128)(2,1)S(1)}, bf16[128,128]{1,0:T(8,128)(2,1)S(1)}, u32[]{:S(2)}, u32[]{:S(2)}) collective-permute-start(bf16[128,128]{1,0:T(8,128)(2,1)S(1)} %get-tuple-element.24.refs_2_.refs_0_), channel_id=1, source_target_pairs={{0,249},{1,248},{2,251},{3,250},{4,253},{5,252},{6,255},{7,254},{8... | collective-permute-start | bytes 98312 | tf_op jit(solution)/shard_map/ppermute | solution.py:236
  44.3 1.5 %phases_0.1.refs_4_.refs_1_.refs_2_ = bf16[2048,256]{1,0:T(8,128)(2,1)S(1)} custom-call(bf16[4,144,128]{2,1,0:T(8,128)(2,1)S(1)} %stack_first.1.refs_1_.refs_10_.refs_0_, f32[1024,3]{1,0:T(8,128)S(1)} %bitcast.11, bf16[128,128]{1,0:T(8,128)(2,1)S(1)} %get-tuple-element.24.refs_2_.refs_0_), custom_call_target="tpu_custom_call" | custom-call | flops 1000000000 | bytes 1048576 | tf_op jit(solution)/shard_map/phases_0/pallas_call | solution.py:52
  45.8 1.5 %phases_1.1.refs_5_.refs_2_.refs_3_ = bf16[2048,256]{1,0:T(8,128)(2,1)S(1)} custom-call(bf16[4,144,128]{2,1,0:T(8,128)(2,1)S(1)} %collective-permute-done.6.refs_1_.refs_0_, f32[1024,3]{1,0:T(8,128)S(1)} %bitcast.12, bf16[128,128]{1,0:T(8,128)(2,1)S(1)} %get-tuple-element.24.refs_2_.refs_0_), custom_call_target="tpu_custom_call" | custom-call | flops 1000000000 | bytes 1048576 | tf_op jit(solution)/shard_map/phases_1/pallas_call | solution.py:52
  47.4 2.1 %collective-permute-start.18 = (bf16[4,128,128]{2,1,0:T(8,128)(2,1)S(1)}, bf16[4,128,128]{2,1,0:T(8,128)(2,1)S(1)}, u32[]{:S(2)}, u32[]{:S(2)}) collective-permute-start(bf16[4,128,128]{2,1,0:T(8,128)(2,1)S(1)} %stack_second.1.refs_2_.refs_0_), channel_id=1, source_target_pairs={{0,4},{1,5},{2,6},{3,7},{4,0},{5,1},{6,2},{7,3},{8,12},{9,13},{10,... | collective-permute-start | bytes 393224 | tf_op jit(solution)/shard_map/ppermute | solution.py:236
  50.9 4.3 %collective-permute-start.15 = (bf16[2,128,128]{2,1,0:T(8,128)(2,1)S(1)}, bf16[2,128,128]{2,1,0:T(8,128)(2,1)S(1)}, u32[]{:S(2)}, u32[]{:S(2)}) collective-permute-start(bf16[2,128,128]{2,1,0:T(8,128)(2,1)S(1)} %slice.47), channel_id=1, source_target_pairs={{0,8},{1,9},{2,10},{3,11},{4,12},{5,13},{6,14},{7,15},{8,0},{9,1},... | collective-permute-start | bytes 196616 | tf_op jit(solution)/shard_map/ppermute | solution.py:236
  55.2 1.5 %phases_3.1.refs_5_.refs_4_ = bf16[2048,256]{1,0:T(8,128)(2,1)S(1)} custom-call(bf16[4,144,128]{2,1,0:T(8,128)(2,1)S(1)} %collective-permute-done.3.refs_1_.refs_0_, f32[1024,3]{1,0:T(8,128)S(1)} %bitcast.13, bf16[4,128,128]{2,1,0:T(8,128)(2,1)S(1)} %stack_second.1.refs_2_.refs_0_), custom_call_target="tpu_custom_call" | custom-call | flops 1000000000 | bytes 1048576 | tf_op jit(solution)/shard_map/phases_3/pallas_call | solution.py:52
  56.7 1.5 %phases_2.1.refs_4_.refs_3_ = bf16[2048,256]{1,0:T(8,128)(2,1)S(1)} custom-call(bf16[4,144,128]{2,1,0:T(8,128)(2,1)S(1)} %collective-permute-done.8.refs_1_.refs_0_, f32[1024,3]{1,0:T(8,128)S(1)} %bitcast.14, bf16[4,128,128]{2,1,0:T(8,128)(2,1)S(1)} %stack_second.1.refs_2_.refs_0_), custom_call_target="tpu_custom_call" | custom-call | flops 1000000000 | bytes 1048576 | tf_op jit(solution)/shard_map/phases_2/pallas_call | solution.py:52
  59.5 1.3 %collective-permute-start.14 = (bf16[2,128,128]{2,1,0:T(8,128)(2,1)S(1)}, bf16[2,128,128]{2,1,0:T(8,128)(2,1)S(1)}, u32[]{:S(2)}, u32[]{:S(2)}) collective-permute-start(bf16[2,128,128]{2,1,0:T(8,128)(2,1)S(1)} %slice.46), channel_id=1, source_target_pairs={{0,8},{1,9},{2,10},{3,11},{4,12},{5,13},{6,14},{7,15},{8,0},{9,1},... | collective-permute-start | bytes 196616 | tf_op jit(solution)/shard_map/ppermute | solution.py:236
  62.1 1.9 %second_3.1 = f32[8,16,128]{2,1,0:T(8,128)} custom-call(s32[8]{0:T(128)S(1)} %concatenate.9.refs_0_, bf16[4,128,128]{2,1,0:T(8,128)(2,1)S(1)} %collective-permute-done.13.refs_1_, bf16[2,128,128]{2,1,0:T(8,128)(2,1)S(1)} %collective-permute-done.14.refs_2_, bf16[1024,768]{1,0:T(8,128)(2,1)S(1)} %get-tuple-element.25.refs_3_, f32[2,8,128]{2,1,0:T(8,128)S(1)} %copy-done.7, ...), custom_call_target="tpu_custom_call" | custom-call | flops 1000000000 | bytes 1048576 | tf_op jit(solution)/shard_map/second_3/pallas_call | solution.py:52
  64.0 4.6 %all-to-all-start = ((f32[8,16,128]{2,1,0:T(8,128)}), f32[8,16,128]{2,1,0:T(8,128)S(1)}, u32[]{:S(2)}, u32[]{:S(2)}) async-start(f32[8,16,128]{2,1,0:T(8,128)} %second_3.1), calls=%async_computation | async-start | bytes 131072 | tf_op jit(solution)/shard_map/all_to_all | solution.py:343
  68.6 9.1 %all-to-all-done.refs_5_ = f32[8,16,128]{2,1,0:T(8,128)S(1)} async-done(((f32[8,16,128]{2,1,0:T(8,128)}), f32[8,16,128]{2,1,0:T(8,128)S(1)}, u32[]{:S(2)}, u32[]{:S(2)}) %all-to-all-start) | async-done | bytes 65568 | tf_op jit(solution)/shard_map/all_to_all | solution.py:343
  77.7 1.2 %copy-done.2 = bf16[2048,256]{1,0:T(8,128)(2,1)S(1)} copy-done((bf16[2048,256]{1,0:T(8,128)(2,1)S(1)}, bf16[2048,256]{1,0:T(8,128)(2,1)}, u32[]{:S(2)}) %copy-start.2) | copy-done | bytes 1048600
  78.9 2.0 %structure.1 = (f32[32,1024]{1,0:T(8,128)S(1)}, f32[16,1024]{1,0:T(8,128)S(1)}) custom-call(s32[8]{0:T(128)S(1)} %fusion.1.refs_0_, bf16[2048,256]{1,0:T(8,128)(2,1)S(1)} %phases_0.1.refs_4_.refs_1_.refs_2_, bf16[2048,256]{1,0:T(8,128)(2,1)S(1)} %phases_1.1.refs_5_.refs_2_.refs_3_, bf16[2048,256]{1,0:T(8,128)(2,1)S(1)} %copy-done.2, ...), custom_call_target="tpu_custom_call" | custom-call | flops 100000000 | bytes 1048576 | tf_op jit(solution)/shard_map/structure/pallas_call | solution.py:52
  80.9 1.8 %collective-permute-start.20 = (f32[32,512]{1,0:T(8,128)S(1)}, f32[32,512]{1,0:T(8,128)S(1)}, u32[]{:S(2)}, u32[]{:S(2)}) collective-permute-start(f32[32,512]{1,0:T(8,128)S(1)} %slice_select_fusion), channel_id=1, source_target_pairs={{0,8},{1,9},{2,10},{3,11},{4,12},{5,13},{6,14},{7,15},{8,0},{9,1},... | collective-permute-start | bytes 196616 | tf_op jit(solution)/shard_map/ppermute | solution.py:236
  83.8 3.4 %collective-permute-start.23 = (f32[32,512]{1,0:T(8,128)S(1)}, f32[32,512]{1,0:T(8,128)S(1)}, u32[]{:S(2)}, u32[]{:S(2)}) collective-permute-start(f32[32,512]{1,0:T(8,128)S(1)} %select_add_fusion), channel_id=1, source_target_pairs={{0,48},{1,49},{2,50},{3,51},{4,52},{5,53},{6,54},{7,55},{8,56},{9,... | collective-permute-start | bytes 196616 | tf_op jit(solution)/shard_map/ppermute | solution.py:236
  87.9 2.1 %collective-permute-done.23 = f32[32,512]{1,0:T(8,128)S(1)} collective-permute-done((f32[32,512]{1,0:T(8,128)S(1)}, f32[32,512]{1,0:T(8,128)S(1)}, u32[]{:S(2)}, u32[]{:S(2)}) %collective-permute-start.23) | collective-permute-done | bytes 65568 | tf_op jit(solution)/shard_map/ppermute | solution.py:236
  90.1 3.0 %collective-permute-start.25 = (f32[32,512]{1,0:T(8,128)S(1)}, f32[32,512]{1,0:T(8,128)S(1)}, u32[]{:S(2)}, u32[]{:S(2)}) collective-permute-start(f32[32,512]{1,0:T(8,128)S(1)} %add_add_fusion.1), channel_id=1, source_target_pairs={{0,128},{1,129},{2,130},{3,131},{4,132},{5,133},{6,134},{7,135},{8... | collective-permute-start | bytes 196616 | tf_op jit(solution)/shard_map/ppermute | solution.py:236
  96.2 4.1 %collective-permute-start.27 = (f32[32,512]{1,0:T(8,128)S(1)}, f32[32,512]{1,0:T(8,128)S(1)}, u32[]{:S(2)}, u32[]{:S(2)}) collective-permute-start(f32[32,512]{1,0:T(8,128)S(1)} %add_add_fusion), channel_id=1, source_target_pairs={{0,8},{1,9},{2,10},{3,11},{4,12},{5,13},{6,14},{7,15},{8,0},{9,1},... | collective-permute-start | bytes 196616 | tf_op jit(solution)/shard_map/ppermute | solution.py:236
  101.2 1.3 %respond.1 = f32[8,24,128]{2,1,0:T(8,128)S(1)} custom-call(s32[8]{0:T(128)S(1)} %fusion.1.refs_0_, f32[1]{0:T(128)} %constant.106.clone.1.refs_1_, bf16[2048,256]{1,0:T(8,128)(2,1)S(1)} %phases_0.1.refs_4_.refs_1_.refs_2_, bf16[2048,256]{1,0:T(8,128)(2,1)S(1)} %phases_1.1.refs_5_.refs_2_.refs_3_, bf16[2048,256]{1,0:T(8,128)(2,1)S(1)} %copy-done.2, ...), custom_call_target="tpu_custom_call" | custom-call | flops 100000000 | bytes 1048576 | tf_op jit(solution)/shard_map/respond/pallas_call | solution.py:52
  102.5 11.7 %all_to_all.10.refs_0_ = f32[8,24,128]{2,1,0:T(8,128)S(1)} all-to-all(f32[8,24,128]{2,1,0:T(8,128)S(1)} %respond.1), channel_id=1, replica_groups=mesh['slab'=32,'kgrp'=8] {'kgrp'}, dimensions={0} | all-to-all | bytes 196608 | tf_op jit(solution)/shard_map/all_to_all | solution.py:372
  (100 shorter events, 18.0 us)
Async XLA Ops:
  2.1 13.7 %collective-permute-start = (bf16[144,128]{1,0:T(8,128)(2,1)S(1)}, bf16[144,128]{1,0:T(8,128)(2,1)S(1)}, u32[]{:S(2)}, u32[]{:S(2)}) collective-permute-start(bf16[144,128]{1,0:T(8,128)(2,1)S(1)} %pack.1.refs_0_), channel_id=1, source_target_pairs={{0,1},{1,0},{2,3},{3,2},{4,5},{5,4},{6,7},{7,6},{8,9},{9,8},{10,11... | collective-permute-start | bytes 110600 | tf_op jit(solution)/shard_map/ppermute | solution.py:236
  9.9 5.9 %collective-permute-start.1 = (bf16[144,128]{1,0:T(8,128)(2,1)S(1)}, bf16[144,128]{1,0:T(8,128)(2,1)S(1)}, u32[]{:S(2)}, u32[]{:S(2)}) collective-permute-start(bf16[144,128]{1,0:T(8,128)(2,1)S(1)} %pack.1.refs_0_), channel_id=1, source_target_pairs={{0,248},{1,249},{2,250},{3,251},{4,252},{5,253},{6,254},{7,255},{8... | collective-permute-start | bytes 110600 | tf_op jit(solution)/shard_map/ppermute | solution.py:236
  11.5 6.5 %collective-permute-start.2 = (bf16[144,128]{1,0:T(8,128)(2,1)S(1)}, bf16[144,128]{1,0:T(8,128)(2,1)S(1)}, u32[]{:S(2)}, u32[]{:S(2)}) collective-permute-start(bf16[144,128]{1,0:T(8,128)(2,1)S(1)} %pack.1.refs_0_), channel_id=1, source_target_pairs={{0,249},{1,248},{2,251},{3,250},{4,253},{5,252},{6,255},{7,254},{8... | collective-permute-start | bytes 110600 | tf_op jit(solution)/shard_map/ppermute | solution.py:236
  14.1 12.6 %copy-start.9 = (f32[3,128]{1,0:T(4,128)S(1)}, f32[3,128]{1,0:T(4,128)}, u32[]{:S(2)}) copy-start(f32[3,128]{1,0:T(4,128)} %refs_1_.1) | copy-start | bytes 4612
  15.8 12.5 %copy-start.7 = (f32[2,8,128]{2,1,0:T(8,128)S(1)}, f32[2,8,128]{2,1,0:T(8,128)}, u32[]{:S(2)}) copy-start(f32[2,8,128]{2,1,0:T(8,128)} %refs_4_.1) | copy-start | bytes 24580
  18.0 9.1 %collective-permute-start.8 = (bf16[4,144,128]{2,1,0:T(8,128)(2,1)S(1)}, bf16[4,144,128]{2,1,0:T(8,128)(2,1)S(1)}, u32[]{:S(2)}, u32[]{:S(2)}) collective-permute-start(bf16[4,144,128]{2,1,0:T(8,128)(2,1)S(1)} %stack_first.1.refs_1_.refs_10_.refs_0_), channel_id=1, source_target_pairs={{0,4},{1,5},{2,6},{3,7},{4,0},{5,1},{6,2},{7,3},{8,12},{9,13},{10,... | collective-permute-start | bytes 442376 | tf_op jit(solution)/shard_map/ppermute | solution.py:236
  21.0 9.2 %collective-permute-start.6 = (bf16[4,144,128]{2,1,0:T(8,128)(2,1)S(1)}, bf16[4,144,128]{2,1,0:T(8,128)(2,1)S(1)}, u32[]{:S(2)}, u32[]{:S(2)}) collective-permute-start(bf16[4,144,128]{2,1,0:T(8,128)(2,1)S(1)} %stack_first.1.refs_1_.refs_10_.refs_0_), channel_id=1, source_target_pairs={{0,6},{1,7},{2,0},{3,1},{4,2},{5,3},{6,4},{7,5},{8,14},{9,15},{10,... | collective-permute-start | bytes 442376 | tf_op jit(solution)/shard_map/ppermute | solution.py:236
  21.9 8.5 %collective-permute-start.3 = (bf16[4,144,128]{2,1,0:T(8,128)(2,1)S(1)}, bf16[4,144,128]{2,1,0:T(8,128)(2,1)S(1)}, u32[]{:S(2)}, u32[]{:S(2)}) collective-permute-start(bf16[4,144,128]{2,1,0:T(8,128)(2,1)S(1)} %stack_first.1.refs_1_.refs_10_.refs_0_), channel_id=1, source_target_pairs={{0,2},{1,3},{2,4},{3,5},{4,6},{5,7},{6,0},{7,1},{8,10},{9,11},{10,... | collective-permute-start | bytes 442376 | tf_op jit(solution)/shard_map/ppermute | solution.py:236
  22.6 5.6 %collective-permute-start.5 = (bf16[2,144,128]{2,1,0:T(8,128)(2,1)S(1)}, bf16[2,144,128]{2,1,0:T(8,128)(2,1)S(1)}, u32[]{:S(2)}, u32[]{:S(2)}) collective-permute-start(bf16[2,144,128]{2,1,0:T(8,128)(2,1)S(1)} %slice.43), channel_id=1, source_target_pairs={{0,8},{1,9},{2,10},{3,11},{4,12},{5,13},{6,14},{7,15},{8,0},{9,1},... | collective-permute-start | bytes 221192 | tf_op jit(solution)/shard_map/ppermute | solution.py:236
  27.0 18.7 %copy-start.3 = (f32[3,1024]{0,1:T(8,128)}, f32[3,1024]{0,1:T(8,128)S(1)}, u32[]{:S(2)}) copy-start(f32[3,1024]{0,1:T(8,128)S(1)} %copy.21) | copy-start | bytes 36868
  27.1 4.9 %collective-permute-start.9 = (bf16[2,144,128]{2,1,0:T(8,128)(2,1)S(1)}, bf16[2,144,128]{2,1,0:T(8,128)(2,1)S(1)}, u32[]{:S(2)}, u32[]{:S(2)}) collective-permute-start(bf16[2,144,128]{2,1,0:T(8,128)(2,1)S(1)} %slice.45), channel_id=1, source_target_pairs={{0,8},{1,9},{2,10},{3,11},{4,12},{5,13},{6,14},{7,15},{8,0},{9,1},... | collective-permute-start | bytes 221192 | tf_op jit(solution)/shard_map/ppermute | solution.py:236
  30.3 3.8 %collective-permute-start.7 = (bf16[2,144,128]{2,1,0:T(8,128)(2,1)S(1)}, bf16[2,144,128]{2,1,0:T(8,128)(2,1)S(1)}, u32[]{:S(2)}, u32[]{:S(2)}) collective-permute-start(bf16[2,144,128]{2,1,0:T(8,128)(2,1)S(1)} %slice.44), channel_id=1, source_target_pairs={{0,8},{1,9},{2,10},{3,11},{4,12},{5,13},{6,14},{7,15},{8,0},{9,1},... | collective-permute-start | bytes 221192 | tf_op jit(solution)/shard_map/ppermute | solution.py:236
  30.4 5.7 %collective-permute-start.4 = (bf16[2,144,128]{2,1,0:T(8,128)(2,1)S(1)}, bf16[2,144,128]{2,1,0:T(8,128)(2,1)S(1)}, u32[]{:S(2)}, u32[]{:S(2)}) collective-permute-start(bf16[2,144,128]{2,1,0:T(8,128)(2,1)S(1)} %slice.42), channel_id=1, source_target_pairs={{0,8},{1,9},{2,10},{3,11},{4,12},{5,13},{6,14},{7,15},{8,0},{9,1},... | collective-permute-start | bytes 221192 | tf_op jit(solution)/shard_map/ppermute | solution.py:236
  38.3 9.0 %collective-permute-start.10 = (bf16[128,128]{1,0:T(8,128)(2,1)S(1)}, bf16[128,128]{1,0:T(8,128)(2,1)S(1)}, u32[]{:S(2)}, u32[]{:S(2)}) collective-permute-start(bf16[128,128]{1,0:T(8,128)(2,1)S(1)} %get-tuple-element.24.refs_2_.refs_0_), channel_id=1, source_target_pairs={{0,1},{1,0},{2,3},{3,2},{4,5},{5,4},{6,7},{7,6},{8,9},{9,8},{10,11... | collective-permute-start | bytes 98312 | tf_op jit(solution)/shard_map/ppermute | solution.py:236
  40.4 6.9 %collective-permute-start.11 = (bf16[128,128]{1,0:T(8,128)(2,1)S(1)}, bf16[128,128]{1,0:T(8,128)(2,1)S(1)}, u32[]{:S(2)}, u32[]{:S(2)}) collective-permute-start(bf16[128,128]{1,0:T(8,128)(2,1)S(1)} %get-tuple-element.24.refs_2_.refs_0_), channel_id=1, source_target_pairs={{0,248},{1,249},{2,250},{3,251},{4,252},{5,253},{6,254},{7,255},{8... | collective-permute-start | bytes 98312 | tf_op jit(solution)/shard_map/ppermute | solution.py:236
  40.4 6.9 %collective-permute-start.12 = (bf16[128,128]{1,0:T(8,128)(2,1)S(1)}, bf16[128,128]{1,0:T(8,128)(2,1)S(1)}, u32[]{:S(2)}, u32[]{:S(2)}) collective-permute-start(bf16[128,128]{1,0:T(8,128)(2,1)S(1)} %get-tuple-element.24.refs_2_.refs_0_), channel_id=1, source_target_pairs={{0,249},{1,248},{2,251},{3,250},{4,253},{5,252},{6,255},{7,254},{8... | collective-permute-start | bytes 98312 | tf_op jit(solution)/shard_map/ppermute | solution.py:236
  47.4 10.8 %collective-permute-start.18 = (bf16[4,128,128]{2,1,0:T(8,128)(2,1)S(1)}, bf16[4,128,128]{2,1,0:T(8,128)(2,1)S(1)}, u32[]{:S(2)}, u32[]{:S(2)}) collective-permute-start(bf16[4,128,128]{2,1,0:T(8,128)(2,1)S(1)} %stack_second.1.refs_2_.refs_0_), channel_id=1, source_target_pairs={{0,4},{1,5},{2,6},{3,7},{4,0},{5,1},{6,2},{7,3},{8,12},{9,13},{10,... | collective-permute-start | bytes 393224 | tf_op jit(solution)/shard_map/ppermute | solution.py:236
  49.4 9.7 %collective-permute-start.16 = (bf16[4,128,128]{2,1,0:T(8,128)(2,1)S(1)}, bf16[4,128,128]{2,1,0:T(8,128)(2,1)S(1)}, u32[]{:S(2)}, u32[]{:S(2)}) collective-permute-start(bf16[4,128,128]{2,1,0:T(8,128)(2,1)S(1)} %stack_second.1.refs_2_.refs_0_), channel_id=1, source_target_pairs={{0,6},{1,7},{2,0},{3,1},{4,2},{5,3},{6,4},{7,5},{8,14},{9,15},{10,... | collective-permute-start | bytes 393224 | tf_op jit(solution)/shard_map/ppermute | solution.py:236
  50.2 9.3 %collective-permute-start.13 = (bf16[4,128,128]{2,1,0:T(8,128)(2,1)S(1)}, bf16[4,128,128]{2,1,0:T(8,128)(2,1)S(1)}, u32[]{:S(2)}, u32[]{:S(2)}) collective-permute-start(bf16[4,128,128]{2,1,0:T(8,128)(2,1)S(1)} %stack_second.1.refs_2_.refs_0_), channel_id=1, source_target_pairs={{0,2},{1,3},{2,4},{3,5},{4,6},{5,7},{6,0},{7,1},{8,10},{9,11},{10,... | collective-permute-start | bytes 393224 | tf_op jit(solution)/shard_map/ppermute | solution.py:236
  50.9 7.4 %collective-permute-start.15 = (bf16[2,128,128]{2,1,0:T(8,128)(2,1)S(1)}, bf16[2,128,128]{2,1,0:T(8,128)(2,1)S(1)}, u32[]{:S(2)}, u32[]{:S(2)}) collective-permute-start(bf16[2,128,128]{2,1,0:T(8,128)(2,1)S(1)} %slice.47), channel_id=1, source_target_pairs={{0,8},{1,9},{2,10},{3,11},{4,12},{5,13},{6,14},{7,15},{8,0},{9,1},... | collective-permute-start | bytes 196616 | tf_op jit(solution)/shard_map/ppermute | solution.py:236
  58.2 2.6 %collective-permute-start.19 = (bf16[2,128,128]{2,1,0:T(8,128)(2,1)S(1)}, bf16[2,128,128]{2,1,0:T(8,128)(2,1)S(1)}, u32[]{:S(2)}, u32[]{:S(2)}) collective-permute-start(bf16[2,128,128]{2,1,0:T(8,128)(2,1)S(1)} %slice.49), channel_id=1, source_target_pairs={{0,8},{1,9},{2,10},{3,11},{4,12},{5,13},{6,14},{7,15},{8,0},{9,1},... | collective-permute-start | bytes 196616 | tf_op jit(solution)/shard_map/ppermute | solution.py:236
  59.2 2.2 %collective-permute-start.17 = (bf16[2,128,128]{2,1,0:T(8,128)(2,1)S(1)}, bf16[2,128,128]{2,1,0:T(8,128)(2,1)S(1)}, u32[]{:S(2)}, u32[]{:S(2)}) collective-permute-start(bf16[2,128,128]{2,1,0:T(8,128)(2,1)S(1)} %slice.48), channel_id=1, source_target_pairs={{0,8},{1,9},{2,10},{3,11},{4,12},{5,13},{6,14},{7,15},{8,0},{9,1},... | collective-permute-start | bytes 196616 | tf_op jit(solution)/shard_map/ppermute | solution.py:236
  59.5 2.5 %collective-permute-start.14 = (bf16[2,128,128]{2,1,0:T(8,128)(2,1)S(1)}, bf16[2,128,128]{2,1,0:T(8,128)(2,1)S(1)}, u32[]{:S(2)}, u32[]{:S(2)}) collective-permute-start(bf16[2,128,128]{2,1,0:T(8,128)(2,1)S(1)} %slice.46), channel_id=1, source_target_pairs={{0,8},{1,9},{2,10},{3,11},{4,12},{5,13},{6,14},{7,15},{8,0},{9,1},... | collective-permute-start | bytes 196616 | tf_op jit(solution)/shard_map/ppermute | solution.py:236
  64.0 13.7 %all-to-all-start = ((f32[8,16,128]{2,1,0:T(8,128)}), f32[8,16,128]{2,1,0:T(8,128)S(1)}, u32[]{:S(2)}, u32[]{:S(2)}) async-start(f32[8,16,128]{2,1,0:T(8,128)} %second_3.1), calls=%async_computation | async-start | bytes 131072 | tf_op jit(solution)/shard_map/all_to_all | solution.py:343
  80.9 2.7 %collective-permute-start.20 = (f32[32,512]{1,0:T(8,128)S(1)}, f32[32,512]{1,0:T(8,128)S(1)}, u32[]{:S(2)}, u32[]{:S(2)}) collective-permute-start(f32[32,512]{1,0:T(8,128)S(1)} %slice_select_fusion), channel_id=1, source_target_pairs={{0,8},{1,9},{2,10},{3,11},{4,12},{5,13},{6,14},{7,15},{8,0},{9,1},... | collective-permute-start | bytes 196616 | tf_op jit(solution)/shard_map/ppermute | solution.py:236
  83.6 3.6 %collective-permute-start.21 = (f32[32,512]{1,0:T(8,128)S(1)}, f32[32,512]{1,0:T(8,128)S(1)}, u32[]{:S(2)}, u32[]{:S(2)}) collective-permute-start(f32[32,512]{1,0:T(8,128)S(1)} %select_add_fusion), channel_id=1, source_target_pairs={{0,16},{1,17},{2,18},{3,19},{4,20},{5,21},{6,22},{7,23},{8,24},{9,... | collective-permute-start | bytes 196616 | tf_op jit(solution)/shard_map/ppermute | solution.py:236
  83.7 4.2 %collective-permute-start.22 = (f32[32,512]{1,0:T(8,128)S(1)}, f32[32,512]{1,0:T(8,128)S(1)}, u32[]{:S(2)}, u32[]{:S(2)}) collective-permute-start(f32[32,512]{1,0:T(8,128)S(1)} %select_add_fusion), channel_id=1, source_target_pairs={{0,32},{1,33},{2,34},{3,35},{4,36},{5,37},{6,38},{7,39},{8,40},{9,... | collective-permute-start | bytes 196616 | tf_op jit(solution)/shard_map/ppermute | solution.py:236
  83.8 6.2 %collective-permute-start.23 = (f32[32,512]{1,0:T(8,128)S(1)}, f32[32,512]{1,0:T(8,128)S(1)}, u32[]{:S(2)}, u32[]{:S(2)}) collective-permute-start(f32[32,512]{1,0:T(8,128)S(1)} %select_add_fusion), channel_id=1, source_target_pairs={{0,48},{1,49},{2,50},{3,51},{4,52},{5,53},{6,54},{7,55},{8,56},{9,... | collective-permute-start | bytes 196616 | tf_op jit(solution)/shard_map/ppermute | solution.py:236
  90.1 4.4 %collective-permute-start.24 = (f32[32,512]{1,0:T(8,128)S(1)}, f32[32,512]{1,0:T(8,128)S(1)}, u32[]{:S(2)}, u32[]{:S(2)}) collective-permute-start(f32[32,512]{1,0:T(8,128)S(1)} %add_add_fusion.1), channel_id=1, source_target_pairs={{0,64},{1,65},{2,66},{3,67},{4,68},{5,69},{6,70},{7,71},{8,72},{9,... | collective-permute-start | bytes 196616 | tf_op jit(solution)/shard_map/ppermute | solution.py:236
  90.1 5.3 %collective-permute-start.25 = (f32[32,512]{1,0:T(8,128)S(1)}, f32[32,512]{1,0:T(8,128)S(1)}, u32[]{:S(2)}, u32[]{:S(2)}) collective-permute-start(f32[32,512]{1,0:T(8,128)S(1)} %add_add_fusion.1), channel_id=1, source_target_pairs={{0,128},{1,129},{2,130},{3,131},{4,132},{5,133},{6,134},{7,135},{8... | collective-permute-start | bytes 196616 | tf_op jit(solution)/shard_map/ppermute | solution.py:236
  93.1 3.1 %collective-permute-start.26 = (f32[32,512]{1,0:T(8,128)S(1)}, f32[32,512]{1,0:T(8,128)S(1)}, u32[]{:S(2)}, u32[]{:S(2)}) collective-permute-start(f32[32,512]{1,0:T(8,128)S(1)} %add_add_fusion.1), channel_id=1, source_target_pairs={{0,192},{1,193},{2,194},{3,195},{4,196},{5,197},{6,198},{7,199},{8... | collective-permute-start | bytes 196616 | tf_op jit(solution)/shard_map/ppermute | solution.py:236
  96.2 5.0 %collective-permute-start.27 = (f32[32,512]{1,0:T(8,128)S(1)}, f32[32,512]{1,0:T(8,128)S(1)}, u32[]{:S(2)}, u32[]{:S(2)}) collective-permute-start(f32[32,512]{1,0:T(8,128)S(1)} %add_add_fusion), channel_id=1, source_target_pairs={{0,8},{1,9},{2,10},{3,11},{4,12},{5,13},{6,14},{7,15},{8,0},{9,1},... | collective-permute-start | bytes 196616 | tf_op jit(solution)/shard_map/ppermute | solution.py:236
  (10 other events, 44.6 us)
